TPU v7x, 256 devices: a whole 4x4x8 slice. The times are simulated.
256 devices in a mesh: rad: 4 (over x), lat: 8 (over y, core), lon: 8 (over z).
Axes of the slice: x: 4, y: 4, z: 8, core: 2. Of those that a mesh axis runs over, the one named last changes fastest.
Arguments:
- forcing: float32 [3, 32, 256, 1024], P(None, 'rad', 'lat', 'lon'), may hold values from -6 to 6
- pressure: float32 [32, 256, 1024], P('rad', 'lat', 'lon'), may hold values from -6 to 6
- viscosity: float32 [32, 256, 1024], P('rad', 'lat', 'lon'), may hold values from 0.01 to 100
- forward_velocity: float32 [3, 32, 256, 1024], P(None, 'rad', 'lat', 'lon'), may hold values from -6 to 6
- coarse_owner: int32 [8, 64, 256], P('rad', 'lat', 'lon'), may hold values from 0 to 1023, as said below
Outputs:
- adjoint_velocity: float32 [3, 32, 256, 1024], P(None, 'rad', 'lat', 'lon')
- pressure_next: float32 [32, 256, 1024], P('rad', 'lat', 'lon')
- viscosity_gradient: float32 [32, 256, 1024], P('rad', 'lat', 'lon')
Inputs may be any that keep to these rules, and one draw needn't show every extreme that they name: `coarse_owner`: aggregates are blocks of 2 x 8 level-two cells across the first two dimensions by one of 32 runs of varied lengths along the third; the runs are the same for all blocks, every aggregate has members, and a new run begins at every multiple of 32 along the third dimension. Aggregate numbers are (block along the first dimension times blocks along the second plus block along the second) times 32 plus the run's number, runs numbered in order along the third dimension starting at cell 0.
All inputs are finite; a program needn't handle non-finite values.
Results may differ from a plain program's by a relative error of at most 0.0003.
Values sent between devices are 32-bit elements; how exact they have to be, the bound alone decides.
A program may use at most 192 MiB of HBM per device.

v0:
```python
import jax
import jax.numpy as jnp
from jax import lax
from jax.sharding import PartitionSpec as P

AX = 2
AY = 8
ZSEG = 32
DEG = 3
CDEG = 8


FINE_LOW = 0.5
FINE_HIGH = 2.0
COARSE_LOW = 0.1
COARSE_HIGH = 2.0


def extended(x, sides, width):
    for axis, dim in sides:
        count, length = (lax.axis_size(axis), x.shape[dim])
        up = [(i, (i + 1) % count) for i in range(count)]
        down = [(j, i) for i, j in up]
        last = lax.slice_in_dim(x, length - width, length, axis=dim)
        leading = lax.slice_in_dim(x, 0, width, axis=dim)
        before = lax.ppermute(last, axis, up)
        after = lax.ppermute(leading, axis, down)
        x = jnp.concatenate([before, x, after], axis=dim)
    return x


def chebyshev(operate, inverse_diag, solution, residual, low, high, degree):
    middle = 0.5 * (high + low)
    spread = 0.5 * (high - low)
    factor = middle / spread
    carry_old = 1.0 / factor
    update = inverse_diag * residual / middle
    solution = solution + update
    for sweep in range(degree - 1):
        residual = residual - operate(update)
        carry_new = 1.0 / (2.0 * factor - carry_old)
        update = carry_new * carry_old * update + 2.0 * carry_new / spread * inverse_diag * residual
        solution = solution + update
        carry_old = carry_new
    return (solution, residual, update)


def stencil(links, diagonal, vector):
    padded = extended(vector, (("rad", 1), ("lat", 2), ("lon", 3)), 1)
    summed = diagonal * vector
    summed = summed - links[0] * padded[:, :-2, 1:-1, 1:-1] - links[1] * padded[:, 2:, 1:-1, 1:-1]
    summed = summed - links[2] * padded[:, 1:-1, :-2, 1:-1] - links[3] * padded[:, 1:-1, 2:, 1:-1]
    summed = summed - links[4] * padded[:, 1:-1, 1:-1, :-2] - links[5] * padded[:, 1:-1, 1:-1, 2:]
    return summed


def coarsen_face(values, direction, side):
    size_x, size_y, size_z = values.shape
    blocks = values.reshape(size_x // 2, 2, size_y // 2, 2, size_z // 2, 2)
    weights = []
    for other in range(3):
        if other == direction:
            weights.append(jnp.array([1.0 - side, float(side)], jnp.float32))
        else:
            weights.append(jnp.ones((2,), jnp.float32))
    scaled = (
        blocks
        * weights[0][None, :, None, None, None, None]
        * weights[1][None, None, None, :, None, None]
        * weights[2][None, None, None, None, None, :]
    )
    return scaled.sum(axis=(1, 3, 5))


def coarsen_level(faces, links):
    new_faces = jnp.stack([coarsen_face(faces[k], k // 2, k % 2) for k in range(6)])
    new_links = jnp.stack([coarsen_face(links[k], k // 2, k % 2) for k in range(6)])
    diagonal = (
        new_faces[0] + new_faces[1] + new_faces[2] + new_faces[3] + new_faces[4] + new_faces[5]
    )
    return (new_faces, new_links, diagonal)


def restrict(vector):
    comps, size_x, size_y, size_z = vector.shape
    return vector.reshape(comps, size_x // 2, 2, size_y // 2, 2, size_z // 2, 2).sum(axis=(2, 4, 6))


def prolong(vector):
    return jnp.repeat(jnp.repeat(jnp.repeat(vector, 2, axis=1), 2, axis=2), 2, axis=3)


def fine_faces(viscosity, neighbours, masks):
    lower_x, upper_x, lower_y, upper_y = masks
    prev_x, next_x, prev_y, next_y, prev_z, next_z = neighbours
    faces = jnp.stack(
        [
            0.5 * (viscosity + lower_x * prev_x),
            0.5 * (viscosity + upper_x * next_x),
            0.5 * (viscosity + lower_y * prev_y),
            0.5 * (viscosity + upper_y * next_y),
            0.5 * (viscosity + prev_z),
            0.5 * (viscosity + next_z),
        ]
    )
    links = jnp.stack(
        [
            faces[0] * lower_x,
            faces[1] * upper_x,
            faces[2] * lower_y,
            faces[3] * upper_y,
            faces[4],
            faces[5],
        ]
    )
    diagonal = faces[0] + faces[1] + faces[2] + faces[3] + faces[4] + faces[5]
    return (faces, links, diagonal)


def galerkin_term(owners, owner_neighbours, links, diagonal, count):
    row_ids = owners.reshape(-1)
    key_list = [row_ids * count + row_ids]
    value_list = [diagonal.reshape(-1)]
    for k in range(6):
        key_list.append(row_ids * count + owner_neighbours[k].reshape(-1))
        value_list.append(-links[k].reshape(-1))
    summed = jax.ops.segment_sum(
        jnp.concatenate(value_list), jnp.concatenate(key_list), num_segments=count * count
    )
    return summed.reshape(count, count)


def aggregate_sums(residual, owners, count):
    flat = residual.reshape(residual.shape[0], -1).T
    return jax.ops.segment_sum(flat, owners.reshape(-1), num_segments=count).T


def strain_sum(forward_grads, adjoint_grads):
    summed = jnp.zeros_like(forward_grads[0][0])
    for d in range(3):
        for e in range(3):
            sym_forward = 0.5 * (forward_grads[e][d] + forward_grads[d][e])
            sym_adjoint = 0.5 * (adjoint_grads[e][d] + adjoint_grads[d][e])
            summed = summed + sym_forward * sym_adjoint
    return summed


def vcycle(levels, coarse, level, right):
    links, diagonal = levels[level]

    def operate(vector):
        return stencil(links, diagonal, vector)

    inverse = 1.0 / diagonal
    solution, residual, update = chebyshev(
        operate, inverse, jnp.zeros_like(right), right, FINE_LOW, FINE_HIGH, DEG
    )
    residual = residual - operate(update)
    if level == 2:
        correction = coarse(residual)
    else:
        correction = prolong(vcycle(levels, coarse, level + 1, restrict(residual)))
    solution = solution + correction
    residual = residual - operate(correction)
    solution, residual, update = chebyshev(
        operate, inverse, solution, residual, FINE_LOW, FINE_HIGH, DEG
    )
    return solution


def per_device(forcing, pressure, viscosity, forward_velocity, coarse_owner):
    cells_x, cells_y, cells_z = viscosity.shape
    total_x = cells_x * lax.axis_size("rad")
    total_y = cells_y * lax.axis_size("lat")
    total_z = cells_z * lax.axis_size("lon")
    global_x = lax.axis_index("rad") * cells_x + jnp.arange(cells_x)
    global_y = lax.axis_index("lat") * cells_y + jnp.arange(cells_y)
    lower_x = (global_x > 0).astype(jnp.float32)[:, None, None]
    upper_x = (global_x < total_x - 1).astype(jnp.float32)[:, None, None]
    lower_y = (global_y > 0).astype(jnp.float32)[None, :, None]
    upper_y = (global_y < total_y - 1).astype(jnp.float32)[None, :, None]
    rims = extended(jnp.stack([viscosity, pressure]), (("rad", 1), ("lat", 2), ("lon", 3)), 1)
    visc_rim = rims[0]
    neighbours = [
        visc_rim[:-2, 1:-1, 1:-1],
        visc_rim[2:, 1:-1, 1:-1],
        visc_rim[1:-1, :-2, 1:-1],
        visc_rim[1:-1, 2:, 1:-1],
        visc_rim[1:-1, 1:-1, :-2],
        visc_rim[1:-1, 1:-1, 2:],
    ]
    faces, links, diagonal = fine_faces(viscosity, neighbours, (lower_x, upper_x, lower_y, upper_y))
    levels = [(links, diagonal)]
    for level in range(2):
        faces, links, diagonal = coarsen_level(faces, links)
        levels.append((links, diagonal))
    owner_rim = extended(coarse_owner, (("rad", 0), ("lat", 1), ("lon", 2)), 1)
    owner_neighbours = [
        owner_rim[:-2, 1:-1, 1:-1],
        owner_rim[2:, 1:-1, 1:-1],
        owner_rim[1:-1, :-2, 1:-1],
        owner_rim[1:-1, 2:, 1:-1],
        owner_rim[1:-1, 1:-1, :-2],
        owner_rim[1:-1, 1:-1, 2:],
    ]
    blocks_x = total_x // 4 // AX
    blocks_y = total_y // 4 // AY
    aggregates = blocks_x * blocks_y * ZSEG
    local_term = galerkin_term(
        coarse_owner, owner_neighbours, levels[2][0], levels[2][1], aggregates
    )
    matrix = lax.psum(local_term, ("rad", "lat", "lon"))
    coarse_inverse = 1.0 / jnp.diagonal(matrix)

    def dense_apply(vector):
        return jnp.dot(vector, matrix, precision=lax.Precision.HIGHEST)

    def coarse(residual):
        right = lax.psum(aggregate_sums(residual, coarse_owner, aggregates), ("rad", "lat", "lon"))
        solution, last, update = chebyshev(
            dense_apply, coarse_inverse, jnp.zeros_like(right), right, COARSE_LOW, COARSE_HIGH, CDEG
        )
        return jnp.take(solution, coarse_owner, axis=1)

    pres_rim = rims[1]
    pressure_grad = jnp.stack(
        [
            pres_rim[2:, 1:-1, 1:-1] * upper_x - pressure,
            pres_rim[1:-1, 2:, 1:-1] * upper_y - pressure,
            pres_rim[1:-1, 1:-1, 2:] - pressure,
        ]
    )
    right = forcing - pressure_grad
    adjoint = vcycle(levels, coarse, 0, right)
    both = extended(
        jnp.concatenate([adjoint, forward_velocity], axis=0),
        (("rad", 1), ("lat", 2), ("lon", 3)),
        1,
    )
    divergence = (
        adjoint[0]
        - lower_x * both[0, :-2, 1:-1, 1:-1]
        + (adjoint[1] - lower_y * both[1, 1:-1, :-2, 1:-1])
        + (adjoint[2] - both[2, 1:-1, 1:-1, :-2])
    )
    raw = pressure - viscosity * divergence
    summed = lax.psum(jnp.sum(raw), ("rad", "lat", "lon"))
    pressure_next = raw - summed / (total_x * total_y * total_z)
    upper = [upper_x, upper_y, jnp.ones((1, 1, 1), jnp.float32)]

    def upper_value(index, direction):
        if direction == 0:
            return both[index, 2:, 1:-1, 1:-1]
        if direction == 1:
            return both[index, 1:-1, 2:, 1:-1]
        return both[index, 1:-1, 1:-1, 2:]

    def gradients(velocity, offset):
        return [
            [upper_value(offset + e, d) * upper[d] - velocity[e] for d in range(3)]
            for e in range(3)
        ]

    viscosity_gradient = (
        2.0 * viscosity * strain_sum(gradients(forward_velocity, 3), gradients(adjoint, 0))
    )
    return (adjoint, pressure_next, viscosity_gradient)


def solution(mesh):
    placed = (
        P(None, "rad", "lat", "lon"),
        P("rad", "lat", "lon"),
        P("rad", "lat", "lon"),
        P(None, "rad", "lat", "lon"),
        P("rad", "lat", "lon"),
    )
    return jax.shard_map(
        per_device,
        mesh=mesh,
        in_specs=placed,
        out_specs=(P(None, "rad", "lat", "lon"), P("rad", "lat", "lon"), P("rad", "lat", "lon")),
        check_vma=False,
    )
```

profile of v0, /device:TPU:1, one launch (start us, length us, event | category | flops | bytes accessed | tf_op | source)
XLA Modules:
  0.0 991.3 jit_solution(8193434760288309515)
XLA Ops:
  12.3 2.6 collective-permute-start.55
  17.4 3.5 collective-permute-start.56
  25.7 4.0 collective-permute-start.59
  37.2 3.3 collective-permute-start.5
  40.5 7.1 collective-permute-done.4
  50.4 9.7 reshape_squeeze_stack.76
  60.2 9.7 reshape_squeeze_stack.78
  69.9 9.7 reshape_squeeze_stack.80
  79.6 9.7 reshape_squeeze_stack.72
  89.3 9.8 reshape_squeeze_stack.74
  100.5 3.0 collective-permute-start.7
  103.5 16.8 %multiply_reduce_fusion.1 = (f32[4,16,64]{2,1,0:T(8,128)S(1)}, f32[4,16,64]{2,1,0:T(8,128)S(1)}, f32[4,16,64]{2,1,0:T(8,128)S(1)}, f32[4,16,64]{2,1,0:T(8,128)}, f32[4,16,64]{2,1,0:T(8,128)}) fusion(f32[4,2,16,2,64,2]{5,4,3,2,1,0:T(8,128)} %reshape_squeeze_stack.78, f32[2]{0:T(128)S(1)} %copy-done.109, f32[4,2,16,2,64,2]{5,4,3,2,1,0:T(8,128)} %reshape_squeeze_stack.80, ...), kind=kLoop, calls=%fused_computation.15 | loop fusion | flops 307200 | bytes 737288 | tf_op jit(solution)/shard_map/reduce_sum | solution.py:72
  120.3 9.7 reshape_squeeze_stack.77
  132.1 4.3 fusion.4
  136.4 9.7 reshape_squeeze_stack.73
  148.7 2.6 collective-permute-start.10
  152.0 4.7 fusion
  156.8 9.7 reshape_squeeze_stack.75
  171.1 2.7 collective-permute-start.13
  173.7 4.7 fusion.2
  178.5 9.7 reshape_squeeze_stack.79
  192.0 4.1 fusion.1
  196.2 9.7 reshape_squeeze_stack.81
  211.6 4.1 fusion.3
  226.7 2.6 multiply_add_fusion.1
  229.7 2.7 collective-permute-start.19
  232.3 2.5 multiply_reduce_fusion.6
  236.5 2.6 collective-permute-start.21
  242.8 2.6 collective-permute-start.23
  251.5 26.5 %reshape.281 = f32[3,4,2,16,2,64,2]{6,5,4,3,2,1,0:T(8,128)} reshape(f32[3,8,32,128]{3,2,1,0:T(8,128)S(1)} %fusion.59) | data formatting | bytes 786432 | tf_op jit(solution)/shard_map/reshape | solution.py:86
  278.0 9.4 reduce_sum.251
  287.6 2.7 collective-permute-start.25
  293.0 3.8 collective-permute-start.27
  298.3 2.7 collective-permute-start.29
  301.2 3.2 collective-permute-done.28
  312.1 3.0 collective-permute-start.33
  328.2 3.1 collective-permute-start.38
  343.6 4.1 reshape.282
  353.6 2.8 collective-permute-start.44
  371.9 4.9 collective-permute-start.51
  377.4 25.2 %scatter_custom_fusion = f32[1048576]{0:T(1024)} fusion(s32[3584]{0:T(1024)} %copy-done.118, f32[3584]{0:T(1024)} %constant_dynamic-update-slice_fusion.9, f32[]{:T(128)} %constant.50.clone.1), kind=kCustom, calls=%fused_computation.19 | custom fusion | flops 3584 | bytes 4194816 | tf_op jit(solution)/shard_map/scatter-add | solution.py:127
  402.6 4.9 reshape.290
  417.4 2.8 collective-permute-start.63
  426.6 4.0 scatter_custom_fusion.1
  430.8 82.1 %psum.22 = f32[3,1024]{1,0:T(4,128)S(1)} all-reduce(f32[3,1024]{1,0:T(4,128)S(1)} %bitcast.346), channel_id=1, replica_groups=mesh['rad'=4,'lat'=8,'lon'=8] {'rad','lat','lon'}, use_global_device_ids=true, to_apply=%region_29.30 | all-reduce | flops 3072 | bytes 24576 | tf_op jit(solution)/shard_map/psum | solution.py:219
  512.8 160.6 %all-reduce.2.cloned.1.call-done = f32[1024,1024]{1,0:T(8,128)} async-done(((f32[1024,1024]{1,0:T(8,128)}), f32[1024,1024]{1,0:T(8,128)}) %all-reduce.2.cloned.1.call-update) | async-done | bytes 4194320 | tf_op jit(solution)/shard_map/psum | solution.py:212
  673.5 18.2 %gather_fusion = f32[1024]{0:T(1024)S(1)} fusion(f32[1024,1024]{1,0:T(8,128)} %all-reduce.2.cloned.1.call-done, s32[1024]{0:T(1024)S(1)} %bitcast.333), kind=kCustom, calls=%fused_computation | custom fusion | bytes 16384 | tf_op jit(solution)/shard_map/jit(diagonal)/cond/branch_0_fun/gather | solution.py:213
  691.7 4.4 multiply_add_fusion.13
  714.2 4.5 collective-permute-start.68
  722.1 2.7 collective-permute-start.71
  736.5 3.5 collective-permute-start.77
  761.9 2.6 collective-permute-start.86
  770.6 3.3 collective-permute-done.88
  778.7 4.3 collective-permute-start.92
  789.0 3.3 collective-permute-done.94
  796.7 4.0 collective-permute-start.98
  807.3 2.8 collective-permute-done.100
  818.6 4.1 collective-permute-start.104
  841.1 2.6 collective-permute-start.110
  854.7 2.6 multiply_add_fusion
  861.9 2.6 collective-permute-start.116
  864.5 3.2 collective-permute-start.117
  887.6 3.7 collective-permute-start.123
  900.9 80.1 %psum.23 = f32[]{:T(128)} all-reduce(f32[]{:T(128)} %get-tuple-element.28), channel_id=1, replica_groups=mesh['rad'=4,'lat'=8,'lon'=8] {'rad','lat','lon'}, use_global_device_ids=true, to_apply=%region_31.32 | all-reduce | flops 1 | bytes 8 | tf_op jit(solution)/shard_map/psum | solution.py:247
  (711 shorter events, 298.2 us)
Async XLA Ops:
  7.2 666.3 %all-reduce.2.cloned.1.call-start = ((), (), s32[]{:S(2)}) async-start(), calls=%async_computation | async-start | bytes 8388608 | tf_op jit(solution)/shard_map/psum | solution.py:212
  8.0 23.6 %collective-permute-start = (f32[2,1,32,128]{3,2,1,0:T(8,128)S(1)}, f32[2,1,32,128]{3,2,1,0:T(8,128)S(1)}, u32[]{:S(2)}, u32[]{:S(2)}) collective-permute-start(f32[2,1,32,128]{3,2,1,0:T(8,128)S(1)} %get-tuple-element.121), channel_id=1, source_target_pairs={{0,64},{64,128},{128,192},{192,0},{1,65},{65,129},{129,193},{193,1... | collective-permute-start | bytes 98312 | tf_op jit(solution)/shard_map/ppermute | solution.py:26
  10.1 21.5 %collective-permute-start.1 = (f32[2,1,32,128]{3,2,1,0:T(8,128)S(1)}, f32[2,1,32,128]{3,2,1,0:T(8,128)S(1)}, u32[]{:S(2)}, u32[]{:S(2)}) collective-permute-start(f32[2,1,32,128]{3,2,1,0:T(8,128)S(1)} %get-tuple-element.122), channel_id=1, source_target_pairs={{64,0},{128,64},{192,128},{0,192},{65,1},{129,65},{193,129},{1,193... | collective-permute-start | bytes 98312 | tf_op jit(solution)/shard_map/ppermute | solution.py:27
  17.4 4.7 collective-permute-start.56
  24.0 7.3 collective-permute-start.58
  25.7 5.6 collective-permute-start.59
  37.2 10.4 %collective-permute-start.4 = (f32[2,10,34,1]{3,0,2,1:T(2,128)S(1)}, f32[2,10,34,1]{3,0,2,1:T(2,128)S(1)}, u32[]{:S(2)}, u32[]{:S(2)}) collective-permute-start(f32[2,10,34,1]{3,0,2,1:T(2,128)S(1)} %get-tuple-element.117), channel_id=1, source_target_pairs={{0,1},{1,2},{2,3},{3,4},{4,5},{5,6},{6,7},{7,0},{8,9},{9,10},{10,1... | collective-permute-start | bytes 8168 | tf_op jit(solution)/shard_map/ppermute | solution.py:26
  37.2 10.4 %collective-permute-start.5 = (f32[2,10,34,1]{3,0,2,1:T(2,128)S(1)}, f32[2,10,34,1]{3,0,2,1:T(2,128)S(1)}, u32[]{:S(2)}, u32[]{:S(2)}) collective-permute-start(f32[2,10,34,1]{3,0,2,1:T(2,128)S(1)} %get-tuple-element.118), channel_id=1, source_target_pairs={{1,0},{2,1},{3,2},{4,3},{5,4},{6,5},{7,6},{0,7},{9,8},{10,9},{11,1... | collective-permute-start | bytes 8168 | tf_op jit(solution)/shard_map/ppermute | solution.py:27
  100.1 29.9 %collective-permute-start.6 = (f32[3,1,32,128]{3,2,1,0:T(8,128)S(1)}, f32[3,1,32,128]{3,2,1,0:T(8,128)S(1)}, u32[]{:S(2)}, u32[]{:S(2)}) collective-permute-start(f32[3,1,32,128]{3,2,1,0:T(8,128)S(1)} %get-tuple-element.115), channel_id=1, source_target_pairs={{0,64},{64,128},{128,192},{192,0},{1,65},{65,129},{129,193},{193,1... | collective-permute-start | bytes 147464 | tf_op jit(solution)/shard_map/ppermute | solution.py:26
  100.5 29.5 %collective-permute-start.7 = (f32[3,1,32,128]{3,2,1,0:T(8,128)S(1)}, f32[3,1,32,128]{3,2,1,0:T(8,128)S(1)}, u32[]{:S(2)}, u32[]{:S(2)}) collective-permute-start(f32[3,1,32,128]{3,2,1,0:T(8,128)S(1)} %get-tuple-element.116), channel_id=1, source_target_pairs={{64,0},{128,64},{192,128},{0,192},{65,1},{129,65},{193,129},{1,193... | collective-permute-start | bytes 147464 | tf_op jit(solution)/shard_map/ppermute | solution.py:27
  130.0 16.1 %collective-permute-start.8 = (f32[3,10,1,128]{3,2,1,0:T(1,128)S(1)}, f32[3,10,1,128]{3,2,1,0:T(1,128)S(1)}, u32[]{:S(2)}, u32[]{:S(2)}) collective-permute-start(f32[3,10,1,128]{3,2,1,0:T(1,128)S(1)} %get-tuple-element.103), channel_id=1, source_target_pairs={{0,8},{8,16},{16,24},{24,32},{32,40},{40,48},{48,56},{56,0},{1,9},... | collective-permute-start | bytes 46088 | tf_op jit(solution)/shard_map/ppermute | solution.py:26
  131.6 14.6 %collective-permute-start.9 = (f32[3,10,1,128]{3,2,1,0:T(1,128)S(1)}, f32[3,10,1,128]{3,2,1,0:T(1,128)S(1)}, u32[]{:S(2)}, u32[]{:S(2)}) collective-permute-start(f32[3,10,1,128]{3,2,1,0:T(1,128)S(1)} %get-tuple-element.104), channel_id=1, source_target_pairs={{8,0},{16,8},{24,16},{32,24},{40,32},{48,40},{56,48},{0,56},{9,1},... | collective-permute-start | bytes 46088 | tf_op jit(solution)/shard_map/ppermute | solution.py:27
  148.7 17.8 %collective-permute-start.10 = (f32[3,10,34,1]{2,3,1,0:T(1,128)S(1)}, f32[3,10,34,1]{2,3,1,0:T(1,128)S(1)}, u32[]{:S(2)}, u32[]{:S(2)}) collective-permute-start(f32[3,10,34,1]{2,3,1,0:T(1,128)S(1)} %copy.930), channel_id=1, source_target_pairs={{0,1},{1,2},{2,3},{3,4},{4,5},{5,6},{6,7},{7,0},{8,9},{9,10},{10,1... | collective-permute-start | bytes 12248 | tf_op jit(solution)/shard_map/ppermute | solution.py:26
  151.6 15.3 %collective-permute-start.11 = (f32[3,10,34,1]{2,3,1,0:T(1,128)S(1)}, f32[3,10,34,1]{2,3,1,0:T(1,128)S(1)}, u32[]{:S(2)}, u32[]{:S(2)}) collective-permute-start(f32[3,10,34,1]{2,3,1,0:T(1,128)S(1)} %copy.931), channel_id=1, source_target_pairs={{1,0},{2,1},{3,2},{4,3},{5,4},{6,5},{7,6},{0,7},{9,8},{10,9},{11,1... | collective-permute-start | bytes 12248 | tf_op jit(solution)/shard_map/ppermute | solution.py:27
  170.5 17.7 %collective-permute-start.12 = (f32[3,1,32,128]{3,2,1,0:T(8,128)S(1)}, f32[3,1,32,128]{3,2,1,0:T(8,128)S(1)}, u32[]{:S(2)}, u32[]{:S(2)}) collective-permute-start(f32[3,1,32,128]{3,2,1,0:T(8,128)S(1)} %get-tuple-element.113), channel_id=1, source_target_pairs={{0,64},{64,128},{128,192},{192,0},{1,65},{65,129},{129,193},{193,1... | collective-permute-start | bytes 147464 | tf_op jit(solution)/shard_map/ppermute | solution.py:26
  171.1 17.1 %collective-permute-start.13 = (f32[3,1,32,128]{3,2,1,0:T(8,128)S(1)}, f32[3,1,32,128]{3,2,1,0:T(8,128)S(1)}, u32[]{:S(2)}, u32[]{:S(2)}) collective-permute-start(f32[3,1,32,128]{3,2,1,0:T(8,128)S(1)} %get-tuple-element.114), channel_id=1, source_target_pairs={{64,0},{128,64},{192,128},{0,192},{65,1},{129,65},{193,129},{1,193... | collective-permute-start | bytes 147464 | tf_op jit(solution)/shard_map/ppermute | solution.py:27
  188.2 17.7 %collective-permute-start.14 = (f32[3,10,1,128]{3,2,1,0:T(1,128)S(1)}, f32[3,10,1,128]{3,2,1,0:T(1,128)S(1)}, u32[]{:S(2)}, u32[]{:S(2)}) collective-permute-start(f32[3,10,1,128]{3,2,1,0:T(1,128)S(1)} %get-tuple-element.101), channel_id=1, source_target_pairs={{0,8},{8,16},{16,24},{24,32},{32,40},{40,48},{48,56},{56,0},{1,9},... | collective-permute-start | bytes 46088 | tf_op jit(solution)/shard_map/ppermute | solution.py:26
  190.7 15.2 %collective-permute-start.15 = (f32[3,10,1,128]{3,2,1,0:T(1,128)S(1)}, f32[3,10,1,128]{3,2,1,0:T(1,128)S(1)}, u32[]{:S(2)}, u32[]{:S(2)}) collective-permute-start(f32[3,10,1,128]{3,2,1,0:T(1,128)S(1)} %get-tuple-element.102), channel_id=1, source_target_pairs={{8,0},{16,8},{24,16},{32,24},{40,32},{48,40},{56,48},{0,56},{9,1},... | collective-permute-start | bytes 46088 | tf_op jit(solution)/shard_map/ppermute | solution.py:27
  208.5 16.7 %collective-permute-start.16 = (f32[3,10,34,1]{2,3,1,0:T(1,128)S(1)}, f32[3,10,34,1]{2,3,1,0:T(1,128)S(1)}, u32[]{:S(2)}, u32[]{:S(2)}) collective-permute-start(f32[3,10,34,1]{2,3,1,0:T(1,128)S(1)} %copy.932), channel_id=1, source_target_pairs={{0,1},{1,2},{2,3},{3,4},{4,5},{5,6},{6,7},{7,0},{8,9},{9,10},{10,1... | collective-permute-start | bytes 12248 | tf_op jit(solution)/shard_map/ppermute | solution.py:26
  210.2 15.3 %collective-permute-start.17 = (f32[3,10,34,1]{2,3,1,0:T(1,128)S(1)}, f32[3,10,34,1]{2,3,1,0:T(1,128)S(1)}, u32[]{:S(2)}, u32[]{:S(2)}) collective-permute-start(f32[3,10,34,1]{2,3,1,0:T(1,128)S(1)} %copy.933), channel_id=1, source_target_pairs={{1,0},{2,1},{3,2},{4,3},{5,4},{6,5},{7,6},{0,7},{9,8},{10,9},{11,1... | collective-permute-start | bytes 12248 | tf_op jit(solution)/shard_map/ppermute | solution.py:27
  229.4 5.5 collective-permute-start.18
  229.7 5.2 collective-permute-start.19
  234.9 4.7 collective-permute-start.20
  242.4 4.8 collective-permute-start.22
  242.8 5.5 collective-permute-start.23
  291.6 6.4 collective-permute-start.26
  293.0 5.1 collective-permute-start.27
  298.2 6.1 collective-permute-start.28
  298.3 6.0 collective-permute-start.29
  305.4 4.9 collective-permute-start.30
  310.2 6.6 collective-permute-start.32
  312.1 4.7 collective-permute-start.33
  317.0 6.3 collective-permute-start.34
  318.5 5.1 collective-permute-start.35
  328.2 6.8 collective-permute-start.38
  335.1 6.1 collective-permute-start.40
  337.4 5.4 collective-permute-start.41
  353.6 7.2 collective-permute-start.44
  360.9 5.0 collective-permute-start.46
  367.0 4.8 collective-permute-start.48
  371.9 35.7 %collective-permute-start.51 = (f32[3,4,1,32]{3,2,1,0:T(1,128)S(1)}, f32[3,4,1,32]{3,2,1,0:T(1,128)S(1)}, u32[]{:S(2)}, u32[]{:S(2)}) collective-permute-start(f32[3,4,1,32]{3,2,1,0:T(1,128)S(1)} %get-tuple-element.195), channel_id=1, source_target_pairs={{8,0},{16,8},{24,16},{32,24},{40,32},{48,40},{56,48},{0,56},{9,1},... | collective-permute-start | bytes 4616 | tf_op jit(solution)/shard_map/ppermute | solution.py:27
  376.8 30.8 %collective-permute-start.50 = (f32[3,4,1,32]{3,2,1,0:T(1,128)S(1)}, f32[3,4,1,32]{3,2,1,0:T(1,128)S(1)}, u32[]{:S(2)}, u32[]{:S(2)}) collective-permute-start(f32[3,4,1,32]{3,2,1,0:T(1,128)S(1)} %get-tuple-element.194), channel_id=1, source_target_pairs={{0,8},{8,16},{16,24},{24,32},{32,40},{40,48},{48,56},{56,0},{1,9},... | collective-permute-start | bytes 4616 | tf_op jit(solution)/shard_map/ppermute | solution.py:26
  421.1 5.1 collective-permute-start.64
  714.2 5.3 collective-permute-start.68
  736.4 5.1 collective-permute-start.76
  736.5 5.0 collective-permute-start.77
  750.7 4.8 collective-permute-start.82
  761.9 5.2 collective-permute-start.86
  767.8 6.1 collective-permute-start.88
  769.6 4.8 collective-permute-start.89
  778.7 6.9 collective-permute-start.92
  786.2 6.1 collective-permute-start.94
  787.1 5.2 collective-permute-start.95
  796.7 6.3 collective-permute-start.98
  804.0 6.2 collective-permute-start.100
  805.1 5.2 collective-permute-start.101
  818.6 6.1 collective-permute-start.104
  836.5 4.5 collective-permute-start.108
  841.1 5.3 collective-permute-start.110
  857.3 4.6 collective-permute-start.114
  861.9 6.5 collective-permute-start.116
  880.5 4.8 collective-permute-start.120
  885.3 6.6 collective-permute-start.122
  895.9 86.4 %collective-permute-start.125 = (f32[6,10,34,1]{2,3,1,0:T(1,128)S(1)}, f32[6,10,34,1]{2,3,1,0:T(1,128)S(1)}, u32[]{:S(2)}, u32[]{:S(2)}) collective-permute-start(f32[6,10,34,1]{2,3,1,0:T(1,128)S(1)} %copy.955), channel_id=1, source_target_pairs={{1,0},{2,1},{3,2},{4,3},{5,4},{6,5},{7,6},{0,7},{9,8},{10,9},{11,1... | collective-permute-start | bytes 24488 | tf_op jit(solution)/shard_map/ppermute | solution.py:27
  (182 other events, 5869.8 us)
Sparse Core Ops, SparseCore 0:
  407.7 265.6 all-reduce.1
where the time goes:
time: 999 us; the launch traced here: 991 us
  waiting for transfers between devices  238 us (24%)
  starting transfers between devices  220 us (22%)
  local copies, waits for them, and re-layouts  220 us (22%)
  blocking collectives  162 us (16%)
  other arithmetic  117 us (12%)
  matrix products  17.1 us (2%)
  between operations  17.1 us (2%)
    psum x1, waiting for transfers between devices, per_device(): matrix = lax.psum(local_term, ('rad', 'lat', 'lon'))  161 us
    ppermute x63, starting transfers between devices, extended(): after = lax.ppermute(leading, axis, down)  123 us
    another operation x20, local copies, waits for them, and re-layouts, coarsen_face(): blocks = values.reshape(size_x // 2, 2, size_y // 2, 2, size_z // 2, 2)  112 us
    ppermute x63, starting transfers between devices, extended(): before = lax.ppermute(last, axis, up)  97.1 us
    psum x1, blocking collectives, coarse(): lax.psum(aggregate_sums(residual, coarse_owner, aggregates), ('rad', 'lat...  82.1 us
    psum x1, blocking collectives, per_device(): summed = lax.psum(jnp.sum(raw), ('rad', 'lat', 'lon'))  80.1 us
    ppermute x63, waiting for transfers between devices, extended(): before = lax.ppermute(last, axis, up)  57.8 us
    reduce_sum x12, other arithmetic, coarsen_face(): return scaled.sum(axis=(1, 3, 5))  42.7 us
  transfers between devices with their start and end apart: 127, of which 66 were waited for; matrix products, arithmetic and copies ran while one was open for 17% of the time, Pallas kernels for 0%

commit v1 on v0

v1 whole, which is shorter than its diff:
```python
import functools

import jax
import jax.numpy as jnp
from jax import lax
from jax.experimental import pallas as pl
from jax.experimental.pallas import tpu as pltpu
from jax.sharding import PartitionSpec as P

AXES = ("rad", "lat", "lon")
SIZES = (4, 8, 8)
MESH = pl.DeviceIdType.MESH
F32 = jnp.float32
HI = lax.Precision.HIGHEST
CDEG = 8
CELLS = 32 * 256 * 1024
LEVELS = ((8, 32, 128), (4, 16, 64), (2, 8, 32))
TOP = 8


def cheb_constants(low, high, degree):
    middle, spread = 0.5 * (high + low), 0.5 * (high - low)
    factor = middle / spread
    old = 1.0 / factor
    steps = []
    for _ in range(degree - 1):
        new = 1.0 / (2.0 * factor - old)
        steps.append((new * old, 2.0 * new / spread))
        old = new
    return 1.0 / middle, steps


FIRST, STEPS = cheb_constants(0.5, 2.0, 3)
COARSE_FIRST, COARSE_STEPS = cheb_constants(0.1, 2.0, CDEG)


def lanes_of(shape):
    return lax.broadcasted_iota(jnp.int32, shape, len(shape) - 1)


def rows_of(shape):
    return lax.broadcasted_iota(jnp.int32, shape, len(shape) - 2)


def block(x, rows):
    return pl.ds(pl.multiple_of(x * rows, 8), rows)


def kernel(
    forcing, pressure, viscosity, forward, owner,
    adjoint, pnext, gradient,
    load, base, fwd, base_z, fwd_z,
    buf0, buf1, buf2, zbuf, faces0, faces1, faces2, links0, links1, links2,
    diag0, diag1, diag2, inv0, inv1, inv2, res0, res1, res2, sol0, sol1, sol2,
    tmp, flat, erows, tile, got1, got2,
    in_sem, send_sem, recv_sem, fsend, frecv, send1, recv1, send2, recv2,
):
    bufs = (buf0, buf1, buf2)
    faces, links = (faces0, faces1, faces2), (links0, links1, links2)
    diags, invs = (diag0, diag1, diag2), (inv0, inv1, inv2)
    ress, sols = (res0, res1, res2), (sol0, sol1, sol2)
    me = tuple(lax.axis_index(a) for a in AXES)
    rad, lat, lon = me

    def device(*steps):
        return tuple(
            lax.rem(m + (s % n), n) if s % n else m for m, s, n in zip(me, steps, SIZES)
        )

    up = [device(1, 0, 0), device(0, 1, 0), device(0, 0, 1)]
    down = [device(-1, 0, 0), device(0, -1, 0), device(0, 0, -1)]
    along = [device(0, 0, k) for k in range(1, 8)]
    across = [device(a, b, 0) for a in range(4) for b in range(8) if a or b]

    own_rows = pl.ds(TOP, 32)
    loads = [
        pltpu.make_async_copy(viscosity, base.at[0, pl.ds(1, 8), own_rows], in_sem.at[0]),
        pltpu.make_async_copy(pressure, base.at[1, pl.ds(1, 8), own_rows], in_sem.at[1]),
        pltpu.make_async_copy(forcing, load, in_sem.at[2]),
        pltpu.make_async_copy(forward, fwd.at[:, pl.ds(1, 8), own_rows], in_sem.at[3]),
    ]
    for copy in loads:
        copy.start()

    barrier = pltpu.get_barrier_semaphore()
    for target in along + across:
        pl.semaphore_signal(barrier, inc=1, device_id=target, device_id_type=MESH)

    def remote(src, dst, ssem, rsem, target):
        return pltpu.make_async_remote_copy(
            src_ref=src, dst_ref=dst, send_sem=ssem, recv_sem=rsem,
            device_id=target, device_id_type=MESH,
        )

    lane8 = lanes_of((8, 128))

    def pack(accs, plane, c, x, level, lows=True, highs=True):
        nx, ny, width = LEVELS[level]
        low, high = accs
        for g in range(ny // 8):
            q = (c * nx + x) * (ny // 8) + g
            turned = pltpu.roll(plane[8 * g : 8 * g + 8], q, 1)
            if lows:
                low = jnp.where(lane8 == q, turned, low)
            if highs:
                high = jnp.where(lane8 == lax.rem(q + width - 1, 128), turned, high)
        return low, high

    zero8 = jnp.zeros((8, 128), F32)

    def merged(level, before, after):
        width = LEVELS[level][2]
        if level == 0:
            return before, after
        left = pltpu.roll(before, 128 - width, 1)
        right = pltpu.roll(after, width, 1)
        return jnp.where((lane8 >= width) & (lane8 < width + 32), right, left)

    def shifted(level, v, halo, c, x):
        nx, ny, width = LEVELS[level]
        groups = ny // 8
        lane = lanes_of((ny, 128))
        q = (c * nx + x) * groups
        if level == 0:
            before, after = halo
            left = [pltpu.roll(before, lax.rem(257 - q - g, 128), 1) for g in range(groups)]
            right = [pltpu.roll(after, lax.rem(255 - q - g, 128), 1) for g in range(groups)]
            low = jnp.where(lane == 0, jnp.concatenate(left, 0), pltpu.roll(v, 1, 1))
            high = jnp.where(lane == 127, jnp.concatenate(right, 0), pltpu.roll(v, 127, 1))
            return low, high
        if halo.shape[0] == 8:
            rim = [pltpu.roll(halo, lax.rem(128 - q - g, 128), 1) for g in range(groups)]
            rim = jnp.concatenate(rim, 0) if groups > 1 else rim[0]
        else:
            rim = jnp.broadcast_to(halo[c : c + 1], (ny, 128))
        wide = jnp.where(lane < width, v, rim)
        return pltpu.roll(wide, 1, 1), pltpu.roll(wide, 127, 1)

    def sends(level, p, buf):
        nx, ny, _ = LEVELS[level]
        rows, planes = pl.ds(TOP, ny), pl.ds(1, nx)
        parts = [
            (buf.at[:, nx, rows], buf.at[:, 0, rows], up[0]),
            (buf.at[:, 1, rows], buf.at[:, nx + 1, rows], down[0]),
            (buf.at[:, planes, pl.ds(TOP + ny - 1, 1)], buf.at[:, planes, pl.ds(TOP - 1, 1)], up[1]),
            (buf.at[:, planes, pl.ds(TOP, 1)], buf.at[:, planes, pl.ds(TOP + ny, 1)], down[1]),
            (zbuf.at[p, 1], zbuf.at[p, 2], up[2]),
            (zbuf.at[p, 0], zbuf.at[p, 3], down[2]),
        ]
        return [
            remote(src, dst, send_sem.at[p, i], recv_sem.at[p, i], target)
            for i, (src, dst, target) in enumerate(parts)
        ]

    turn = [0]

    def exchange(level, accs, buf=None):
        p = turn[0] % 2
        turn[0] += 1
        zbuf[p, 0], zbuf[p, 1] = accs
        copies = sends(level, p, bufs[level].at[p] if buf is None else buf)
        for copy in copies:
            copy.start()

        def finish():
            for copy in copies:
                copy.wait()
            return merged(level, zbuf[p, 2], zbuf[p, 3])

        return finish

    def parity():
        return turn[0] % 2

    for copy in loads[:2]:
        copy.wait()

    def pack_base(x, accs):
        for c in range(2):
            accs = pack(accs, base[c, x + 1, own_rows, :], c, x, 0)
        return accs

    accs = lax.fori_loop(0, 8, pack_base, (zero8, zero8))
    pl.semaphore_wait(barrier, len(along) + len(across))
    finish = exchange(0, accs, base)
    loads[3].wait()

    def pack_fwd(x, accs):
        for c in range(3):
            accs = pack(accs, fwd[c, x + 1, own_rows, :], c, x, 0, highs=False)
        return accs

    fwd_z[0] = lax.fori_loop(0, 8, pack_fwd, (zero8, zero8))[0]
    fwd_parts = [
        (fwd.at[:, 1, own_rows], fwd.at[:, 9, own_rows], down[0]),
        (fwd.at[:, pl.ds(1, 8), pl.ds(TOP, 1)], fwd.at[:, pl.ds(1, 8), pl.ds(TOP + 32, 1)], down[1]),
        (fwd_z.at[0], fwd_z.at[1], down[2]),
    ]
    fwd_copies = [
        remote(src, dst, fsend.at[i], frecv.at[i], target)
        for i, (src, dst, target) in enumerate(fwd_parts)
    ]
    for copy in fwd_copies:
        copy.start()

    grid_row, grid_lane = rows_of((128, 128)), lanes_of((128, 128))
    pair = (grid_row // 2 == grid_lane).astype(F32)
    pick = [(grid_row == 2 * grid_lane + s).astype(F32) for s in range(2)]
    spread = (grid_row == grid_lane // 2).astype(F32)

    def times(a, b):
        return jnp.dot(a, b, precision=HI, preferred_element_type=F32)

    def edge(x, side, nx):
        at_edge = (rad == 0) & (x == 0) if side == 0 else (rad == 3) & (x == nx - 1)
        return jnp.where(at_edge, 0.0, 1.0).astype(F32)

    def edge_rows(side, ny):
        row = rows_of((ny, 128))
        at_edge = (lat == 0) & (row == 0) if side == 0 else (lat == 7) & (row == ny - 1)
        return jnp.where(at_edge, 0.0, 1.0).astype(F32)

    def finish_level(level, x, six):
        nx, ny, width = LEVELS[level]
        at = block(x, ny)
        for k in range(6):
            if k < 2:
                link = six[k] * edge(x, k, nx)
            elif k < 4:
                link = six[k] * edge_rows(k - 2, ny)
            else:
                link = six[k]
            links[level][k, at, :] = link
        total = six[0] + six[1] + six[2] + six[3] + six[4] + six[5]
        diags[level][at, :] = total
        lane = lanes_of((ny, 128))
        invs[level][at, :] = jnp.where(lane < width, 1.0 / jnp.where(lane < width, total, 1.0), 0.0)

    loads[2].wait()
    halo = finish()

    def setup_plane(x, accs):
        v = base[0, x + 1, own_rows, :]
        low_z, high_z = shifted(0, v, halo, 0, x)
        six = [
            0.5 * (v + edge(x, 0, 8) * base[0, x, own_rows, :]),
            0.5 * (v + edge(x, 1, 8) * base[0, x + 2, own_rows, :]),
            0.5 * (v + edge_rows(0, 32) * base[0, x + 1, pl.ds(TOP - 1, 32), :]),
            0.5 * (v + edge_rows(1, 32) * base[0, x + 1, pl.ds(TOP + 1, 32), :]),
            0.5 * (v + low_z),
            0.5 * (v + high_z),
        ]
        at = block(x, 32)
        for k in range(6):
            faces0[k, at, :] = six[k]
        finish_level(0, x, six)
        p = base[1, x + 1, own_rows, :]
        _, high_p = shifted(0, p, halo, 1, x)
        grads = [
            base[1, x + 2, own_rows, :] * edge(x, 1, 8) - p,
            base[1, x + 1, pl.ds(TOP + 1, 32), :] * edge_rows(1, 32) - p,
            high_p - p,
        ]
        for c in range(3):
            right = load[c, x] - grads[c]
            res0[c, at, :] = right
            update = inv0[at, :] * right * FIRST
            sol0[c, at, :] = update
            buf0[1, c, x + 1, own_rows, :] = update
            accs = pack(accs, update, c, x, 0)
        return accs

    start = lax.fori_loop(0, 8, setup_plane, (zero8, zero8))

    def coarsen(level):
        nx, ny, _ = LEVELS[level]
        half_x, half_y = nx // 2, ny // 2
        n = half_x * half_y
        fine = faces[level]
        for k in range(6):
            way, side = k // 2, k % 2

            def one(x, carry):
                if way == 0:
                    plane = fine[k, block(2 * x + side, ny), :]
                else:
                    plane = fine[k, block(2 * x, ny), :] + fine[k, block(2 * x + 1, ny), :]
                tmp[0, pl.ds(0, ny), :] = plane
                even = tmp[0, pl.ds(0, half_y, 2), :]
                odd = tmp[0, pl.ds(1, half_y, 2), :]
                both = (even, odd)[side] if way == 1 else even + odd
                flat[k, block(x, half_y), :] = both
                return carry

            lax.fori_loop(0, half_x, one, 0)
            along_z = pick[side] if way == 2 else pair
            faces[level + 1][k] = times(flat[k, :n, :], along_z)

        def store(x, carry):
            at = block(x, half_y)
            finish_level(level + 1, x, [faces[level + 1][k, at, :] for k in range(6)])
            return carry

        lax.fori_loop(0, half_x, store, 0)

    def sweep(level, p, halo, step, initial=False, emit=None, last=False):
        nx, ny, _ = LEVELS[level]
        buf, link, res, sol = bufs[level], links[level], ress[level], sols[level]

        def plane(x, accs):
            at = block(x, ny)
            diag, inv = diags[level][at, :], invs[level][at, :]
            ls = [link[k, at, :] for k in range(6)]
            for c in range(3):
                v = buf[p, c, x + 1, pl.ds(TOP, ny), :]
                low_z, high_z = shifted(level, v, halo, c, x)
                total = diag * v - ls[0] * buf[p, c, x, pl.ds(TOP, ny), :]
                total = total - ls[1] * buf[p, c, x + 2, pl.ds(TOP, ny), :]
                total = total - ls[2] * buf[p, c, x + 1, pl.ds(TOP - 1, ny), :]
                total = total - ls[3] * buf[p, c, x + 1, pl.ds(TOP + 1, ny), :]
                total = total - ls[4] * low_z - ls[5] * high_z
                r = res[c, at, :] - total
                if step is None:
                    res[c, at, :] = r
                    continue
                if initial:
                    update = FIRST * inv * r
                    after = sol[c, at, :] + v + update
                else:
                    update = step[0] * v + step[1] * inv * r
                    after = sol[c, at, :] + update
                sol[c, at, :] = after
                if last:
                    accs = emit(accs, after, c, x, at)
                else:
                    res[c, at, :] = r
                    buf[1 - p, c, x + 1, pl.ds(TOP, ny), :] = update
                    accs = pack(accs, update, c, x, level)
            return accs

        init = (zero8, zero8) if emit is None or not last else (zero8, zero8, zero8)
        return lax.fori_loop(0, nx, plane, init)

    def smooth_down(level, accs, between=None):
        for step in (STEPS[0], STEPS[1], None):
            p = parity()
            finish = exchange(level, accs)
            if between is not None:
                between()
                between = None
            accs = sweep(level, p, finish(), step)

    def restrict(level):
        nx, ny, _ = LEVELS[level]
        half_x, half_y = nx // 2, ny // 2
        n = half_x * half_y
        res = ress[level]
        for c in range(3):
            def one(x, carry):
                plane = res[c, block(2 * x, ny), :] + res[c, block(2 * x + 1, ny), :]
                tmp[0, pl.ds(0, ny), :] = plane
                even = tmp[0, pl.ds(0, half_y, 2), :]
                flat[c, block(x, half_y), :] = even + tmp[0, pl.ds(1, half_y, 2), :]
                return carry

            lax.fori_loop(0, half_x, one, 0)
            ress[level + 1][c] = times(flat[c, :n, :], pair)
        p = parity()

        def first(x, accs):
            at = block(x, half_y)
            for c in range(3):
                update = FIRST * invs[level + 1][at, :] * ress[level + 1][c, at, :]
                sols[level + 1][c, at, :] = update
                bufs[level + 1][p, c, x + 1, pl.ds(TOP, half_y), :] = update
                accs = pack(accs, update, c, x, level + 1)
            return accs

        return lax.fori_loop(0, half_x, first, (zero8, zero8))

    def prolong(level):
        nx, ny, _ = LEVELS[level]
        half_x, half_y = nx // 2, ny // 2
        p = parity()
        buf = bufs[level]
        for c in range(3):
            flat[c, : half_x * half_y, :] = times(sols[level + 1][c], spread)

        def one(x, accs):
            for c in range(3):
                coarse = flat[c, block(x, half_y), :]
                tmp[0, pl.ds(0, half_y, 2), :] = coarse
                tmp[0, pl.ds(1, half_y, 2), :] = coarse
                fine = tmp[0, pl.ds(0, ny), :]
                for s in range(2):
                    buf[p, c, 2 * x + 1 + s, pl.ds(TOP, ny), :] = fine
                    accs = pack(accs, fine, c, 2 * x + s, level)
            return accs

        return lax.fori_loop(0, half_x, one, (zero8, zero8))

    def gather(use):
        first = [
            remote(tile.at[use, 0], got1.at[use, lon], send1.at[use, i], recv1.at[use, i], target)
            for i, target in enumerate(along)
        ]
        second = [
            remote(tile.at[use, 1], got2.at[use, rad, block(lat, 8)], send2.at[use, i], recv2.at[use, i], target)
            for i, target in enumerate(across)
        ]

        def begin(value):
            tile[use, 0] = value
            got1[use, lon] = value
            for copy in first:
                copy.start()

        def middle():
            for copy in first:
                copy.wait()
            total = got1[use, 0]
            for k in range(1, 8):
                total = total + got1[use, k]
            tile[use, 1] = total
            got2[use, rad, block(lat, 8), :] = total
            for copy in second:
                copy.start()

        def end():
            for copy in second:
                copy.wait()

        return begin, middle, end

    runs = jnp.bitwise_and(owner[0:1, :], 31)
    lane1 = lanes_of((1, 128))
    place = jnp.where(lane1 < 32, runs + 32 * rad, -1)
    member = (grid_row == jnp.broadcast_to(place, (128, 128))).astype(F32)

    def to_runs(rows):
        return lax.dot_general(
            rows, member, (((1,), (1,)), ((), ())), precision=HI, preferred_element_type=F32
        )

    def stacked(rows):
        out = zero8
        row8 = rows_of((8, 128))
        for i, row in enumerate(rows):
            out = jnp.where(row8 == i, jnp.broadcast_to(row, (8, 128)), out)
        return out

    def rowsum(plane):
        return jnp.sum(plane, axis=0, keepdims=True)

    def coarse_solve():
        begin, middle, end = gather(0)
        f = faces2
        here = jnp.where(lane1 < 32, runs, -1)
        first_cell = (lane1 == 0) | (here != pltpu.roll(jnp.broadcast_to(here, (8, 128)), 1, 1)[0:1])
        last_cell = (lane1 == 31) | (here != pltpu.roll(jnp.broadcast_to(here, (8, 128)), 127, 1)[0:1])
        sides = [
            rowsum(f[0, 0:8, :]),
            rowsum(f[1, 8:16, :]),
            f[2, 0:1, :] + f[2, 8:9, :],
            f[3, 7:8, :] + f[3, 15:16, :],
            jnp.where(first_cell, rowsum(f[4, 0:8, :] + f[4, 8:16, :]), 0.0),
            jnp.where(last_cell, rowsum(f[5, 0:8, :] + f[5, 8:16, :]), 0.0),
        ]
        whole = sides[0] + sides[1] + sides[2] + sides[3] + sides[4] + sides[5]
        rights = [rowsum(res2[c, 0:8, :] + res2[c, 8:16, :]) for c in range(3)]
        begin(to_runs(stacked(rights + [sides[0], sides[2], sides[4], whole])))
        middle()
        end()

        def all_of(i):
            out = got2[0, 0, pl.ds(i, 8, 8), :]
            for k in range(1, 4):
                out = out + got2[0, k, pl.ds(i, 8, 8), :]
            return out

        row8 = rows_of((8, 128))
        wrap = jnp.bitwise_and(lane8, 31)

        def lower_z(v):
            return jnp.where(wrap == 0, pltpu.roll(v, 97, 1), pltpu.roll(v, 1, 1))

        def upper_z(v):
            return jnp.where(wrap == 31, pltpu.roll(v, 31, 1), pltpu.roll(v, 127, 1))

        link_x = jnp.where(lane8 < 32, 0.0, all_of(3))
        link_y = jnp.where(row8 == 0, 0.0, all_of(4))
        link_z = all_of(5)
        link_xu, link_yu, link_zu = pltpu.roll(link_x, 96, 1), pltpu.roll(link_y, 7, 0), upper_z(link_z)
        diagonal = all_of(6)
        inverse = 1.0 / diagonal

        def operate(v):
            out = diagonal * v - link_x * pltpu.roll(v, 32, 1) - link_xu * pltpu.roll(v, 96, 1)
            out = out - link_y * pltpu.roll(v, 1, 0) - link_yu * pltpu.roll(v, 7, 0)
            return out - link_z * lower_z(v) - link_zu * upper_z(v)

        rs = [all_of(c) for c in range(3)]
        ds = [inverse * r * COARSE_FIRST for r in rs]
        es = list(ds)
        for a, b in COARSE_STEPS:
            rs = [r - operate(d) for r, d in zip(rs, ds)]
            ds = [a * d + b * inverse * r for r, d in zip(rs, ds)]
            es = [e + d for e, d in zip(es, ds)]
        for c in range(3):
            erows[c] = es[c]
            erows[3 + c] = lower_z(es[c])
            erows[6 + c] = upper_z(es[c])

        def row_of(i, at):
            return erows[i, pl.ds(at, 1), :]

        below, above = lax.rem(lat + 7, 8), lax.rem(lat + 1, 8)
        kinds = []
        for c in range(3):
            mid = row_of(c, lat)
            wide = jnp.broadcast_to(mid, (8, 128))
            kinds.append(to_columns(stacked([
                mid, row_of(3 + c, lat), row_of(6 + c, lat), row_of(c, below), row_of(c, above),
                pltpu.roll(wide, 32, 1)[0:1], pltpu.roll(wide, 96, 1)[0:1],
            ])))
        p = parity()
        rims = []
        for c in range(3):
            k = kinds[c]
            own = jnp.broadcast_to(k[0:1], (8, 128))
            for x in range(2):
                buf2[p, c, 1 + x, pl.ds(TOP, 8), :] = own
                buf2[p, c, 1 + x, pl.ds(TOP - 1, 1), :] = k[3:4]
                buf2[p, c, 1 + x, pl.ds(TOP + 8, 1), :] = k[4:5]
            buf2[p, c, 0, pl.ds(TOP, 8), :] = jnp.broadcast_to(k[5:6], (8, 128))
            buf2[p, c, 3, pl.ds(TOP, 8), :] = jnp.broadcast_to(k[6:7], (8, 128))
            left = pltpu.roll(jnp.broadcast_to(k[1:2], (8, 128)), 127, 1)
            right = pltpu.roll(jnp.broadcast_to(k[2:3], (8, 128)), 1, 1)
            rims.append(jnp.where(lane1 == 127, left[0:1], right[0:1]))
        return p, jnp.concatenate(rims, 0)

    def to_columns(rows):
        return times(rows, member)

    def smooth_up(level, accs, emit=None):
        for i, step in enumerate(STEPS):
            p = parity()
            last = i == len(STEPS) - 1
            halo = exchange(level, accs)()
            accs = sweep(level, p, halo, step, emit=emit, last=last)
        return accs

    def nothing(accs, after, c, x, at):
        return accs

    def coarsen_all():
        coarsen(0)
        coarsen(1)

    smooth_down(0, start, coarsen_all)
    smooth_down(1, restrict(0))
    smooth_down(2, restrict(1))
    p, rim = coarse_solve()
    turn[0] += 1
    accs = sweep(2, p, rim, True, initial=True)
    smooth_up(2, accs, nothing)
    for level in (1, 0):
        accs = prolong(level)
        p = parity()
        halo = exchange(level, accs)()
        accs = sweep(level, p, halo, True, initial=True)
        if level == 1:
            smooth_up(1, accs, nothing)
    final = parity()

    def emit(accs, after, c, x, at):
        adjoint[c, x] = after
        buf0[final, c, x + 1, own_rows, :] = after
        low, high, total = accs
        low, high = pack((low, high), after, c, x, 0)
        v = base[0, x + 1, own_rows, :]
        part = 2.0 * (faces0[2 * c + 1, at, :] - v) * after
        if c == 0:
            part = part + base[1, x + 1, own_rows, :]
        total = total + (part[0:8] + part[8:16] + part[16:24] + part[24:32])
        return low, high, total

    low, high, partial = smooth_up(0, accs, emit)

    begin, middle, end = gather(1)
    finish = exchange(0, (low, high))
    begin(partial)
    for copy in fwd_copies:
        copy.wait()
    middle()
    halo = finish()
    fwd_halo = fwd_z[1]
    lane32 = lanes_of((32, 128))

    def outputs(x, carry):
        at = block(x, 32)
        v = base[0, x + 1, own_rows, :]
        keep_x, keep_y = edge(x, 1, 8), edge_rows(1, 32)
        ga, gf = [], []
        us = []
        for c in range(3):
            u = buf0[final, c, x + 1, own_rows, :]
            low_z, high_z = shifted(0, u, halo, c, x)
            ga.append([
                buf0[final, c, x + 2, own_rows, :] * keep_x - u,
                buf0[final, c, x + 1, pl.ds(TOP + 1, 32), :] * keep_y - u,
                high_z - u,
            ])
            us.append((u, low_z))
            w = fwd[c, x + 1, own_rows, :]
            q = (c * 8 + x) * 4
            right = [pltpu.roll(fwd_halo, lax.rem(255 - q - g, 128), 1) for g in range(4)]
            high_w = jnp.where(lane32 == 127, jnp.concatenate(right, 0), pltpu.roll(w, 127, 1))
            gf.append([
                fwd[c, x + 2, own_rows, :] * keep_x - w,
                fwd[c, x + 1, pl.ds(TOP + 1, 32), :] * keep_y - w,
                high_w - w,
            ])
        divergence = (
            us[0][0] - edge(x, 0, 8) * buf0[final, 0, x, own_rows, :]
            + (us[1][0] - edge_rows(0, 32) * buf0[final, 1, x + 1, pl.ds(TOP - 1, 32), :])
            + (us[2][0] - us[2][1])
        )
        pnext[x] = base[1, x + 1, own_rows, :] - v * divergence
        summed = gf[0][0] * ga[0][0] + gf[1][1] * ga[1][1] + gf[2][2] * ga[2][2]
        for d, e in ((0, 1), (0, 2), (1, 2)):
            summed = summed + 0.5 * (gf[e][d] + gf[d][e]) * (ga[e][d] + ga[d][e])
        gradient[x] = 2.0 * v * summed
        return carry

    lax.fori_loop(0, 8, outputs, 0)
    end()
    total = zero8
    for a in range(4):
        for b in range(8):
            total = total + got2[1, a, 8 * b : 8 * b + 8, :]
    mean = jnp.sum(total) / CELLS

    def shift(x, carry):
        pnext[x] = pnext[x] - mean
        return carry

    lax.fori_loop(0, 8, shift, 0)


def per_device(forcing, pressure, viscosity, forward, owner):
    vmem, anywhere = pl.BlockSpec(memory_space=pltpu.VMEM), pl.BlockSpec(memory_space=pl.ANY)
    first_row = jnp.pad(owner[0, 0:1, :], ((0, 0), (0, 96)))
    f32 = lambda *shape: pltpu.VMEM(shape, F32)
    padded = [f32(2, 3, nx + 2, ny + 16, 128) for nx, ny, _ in LEVELS]
    six = [f32(6, nx * ny, 128) for nx, ny, _ in LEVELS]
    one = [f32(nx * ny, 128) for nx, ny, _ in LEVELS]
    three = [f32(3, nx * ny, 128) for nx, ny, _ in LEVELS]
    dma = lambda *shape: pltpu.SemaphoreType.DMA(shape)
    return pl.pallas_call(
        kernel,
        out_shape=(
            jax.ShapeDtypeStruct((3, 8, 32, 128), F32),
            jax.ShapeDtypeStruct((8, 32, 128), F32),
            jax.ShapeDtypeStruct((8, 32, 128), F32),
        ),
        in_specs=[anywhere] * 4 + [vmem],
        out_specs=(vmem, vmem, vmem),
        scratch_shapes=[
            f32(3, 8, 32, 128), f32(2, 10, 48, 128), f32(3, 10, 48, 128), f32(1, 8, 128), f32(2, 8, 128),
            *padded, f32(2, 4, 8, 128), *six, *six, *one, *one, *three, *three,
            f32(1, 32, 128), f32(6, 64, 128), f32(9, 8, 128), f32(2, 2, 8, 128),
            f32(2, 8, 8, 128), f32(2, 4, 64, 128),
            dma(4), dma(2, 6), dma(2, 6), dma(3), dma(3), dma(2, 7), dma(2, 7), dma(2, 31), dma(2, 31),
        ],
        compiler_params=pltpu.CompilerParams(
            collective_id=0, has_side_effects=True, vmem_limit_bytes=40 * 1024 * 1024
        ),
    )(forcing, pressure, viscosity, forward, first_row)


def solution(mesh):
    placed = (
        P(None, "rad", "lat", "lon"),
        P("rad", "lat", "lon"),
        P("rad", "lat", "lon"),
        P(None, "rad", "lat", "lon"),
        P("rad", "lat", "lon"),
    )
    return jax.shard_map(
        per_device,
        mesh=mesh,
        in_specs=placed,
        out_specs=(P(None, "rad", "lat", "lon"), P("rad", "lat", "lon"), P("rad", "lat", "lon")),
        check_vma=False,
    )
```

time: 999 us -> 126 us (0.13)
  waiting for transfers between devices: 238 us -> 0 us
  starting transfers between devices: 220 us -> 0 us
  local copies, waits for them, and re-layouts: 220 us -> 6.55 us
  blocking collectives: 162 us -> 0 us
  Pallas kernels: 0 us -> 118 us
  other arithmetic: 117 us -> 0 us
  matrix products: 17.1 us -> 0 us
  between operations: 17.1 us -> 0.64 us
    ppermute x126 -> x0, starting transfers between devices: 220 us -> none  [the longest x63 123 us: extended(): after = lax.ppermute(leading, axis, down)]
    psum x2 -> x0, blocking collectives: 162 us -> none  [the longest x1 82.1 us: coarse(): lax.psum(aggregate_sums(residual, coarse_owner, aggregates), ('rad', 'lat...]
    psum x1 -> x0, waiting for transfers between devices: 161 us -> none  [per_device(): matrix = lax.psum(local_term, ('rad', 'lat', 'lon'))]
    pallas_call x0 -> x1, Pallas kernels: none -> 118 us  [per_device(): pl.pallas_call(kernel, out_shape=(jax.ShapeDtypeStruct((3, 8, 32, 128), F...]
    another operation x20 -> x0, local copies, waits for them, and re-layouts: 112 us -> none  [coarsen_face(): blocks = values.reshape(size_x // 2, 2, size_y // 2, 2, size_z // 2, 2)]
    ppermute x126 -> x0, waiting for transfers between devices: 77.1 us -> none  [the longest x63 57.8 us: extended(): before = lax.ppermute(last, axis, up)]
    reduce_sum x15 -> x0, other arithmetic: 54.6 us -> none  [the longest x12 42.7 us: coarsen_face(): return scaled.sum(axis=(1, 3, 5))]
    reshape x15 -> x0, local copies, waits for them, and re-layouts: 39.5 us -> none  [the longest x2 30.6 us: restrict(): vector.reshape(comps, size_x // 2, 2, size_y // 2, 2, size_z // 2, 2)]
  transfers between devices with their start and end apart: 127 -> 0, of which waited for: 66 -> 0; matrix products, arithmetic and copies ran while one was open for 17% -> 0% of each run, Pallas kernels for 0% -> 0%
where the time goes in v1:
time: 126 us; the launch traced here: 125 us
  Pallas kernels  118 us (94%)
  local copies, waits for them, and re-layouts  6.55 us (5%)
    pallas_call x1, Pallas kernels, per_device(): pl.pallas_call(kernel, out_shape=(jax.ShapeDtypeStruct((3, 8, 32, 128), F...  118 us
    unnamed x11, local copies, waits for them, and re-layouts  5.86 us

profile of v1, /device:TPU:1, one launch (start us, length us, event | category | flops | bytes accessed | tf_op | source)
XLA Modules:
  0.0 125.3 jit_solution(5568210632347385622)
XLA Ops:
  0.6 0.7 slice_bitcast_fusion
  1.3 0.0 copy-start
  1.3 1.0 copy-done
  2.3 0.0 copy-start.1
  2.3 1.0 copy-done.1
  3.3 0.0 copy-start.2
  3.3 0.9 copy-done.2
  4.2 0.0 copy-start.3
  4.2 0.9 copy-done.3
  5.1 118.2 %shard_map.76 = (f32[3,8,32,128]{3,2,1,0:T(8,128)S(1)}, f32[8,32,128]{2,1,0:T(8,128)S(1)}, f32[8,32,128]{2,1,0:T(8,128)S(1)}) custom-call(f32[3,8,32,128]{3,2,1,0:T(8,128)S(1)} %copy-done, f32[8,32,128]{2,1,0:T(8,128)S(1)} %copy-done.2, f32[8,32,128]{2,1,0:T(8,128)S(1)} %copy-done.3, f32[3,8,32,128]{3,2,1,0:T(8,128)S(1)} %copy-done.1, s32[1,128]{1,0:T(1,128)S(1)} %pad.4.owner), custom_call_target="tpu_custom_call" | custom-call | tf_op jit(solution)/shard_map/pallas_call | solution.py:660
  123.3 0.7 copy.11
  124.0 0.7 copy.12
  124.7 0.7 copy.13
  (1 shorter events, 0.0 us)
Async XLA Ops:
  1.3 1.0 copy-start
  2.3 1.0 copy-start.1
  3.3 0.9 copy-start.2
  4.2 0.9 copy-start.3

commit v2 on v1

v2 whole, which is shorter than its diff:
```python
import jax
import jax.numpy as jnp
from jax import lax
from jax.experimental import pallas as pl
from jax.experimental.pallas import tpu as pltpu
from jax.sharding import PartitionSpec as P

AXES = ("rad", "lat", "lon")
SIZES = (4, 8, 8)
MESH = pl.DeviceIdType.MESH
F32 = jnp.float32
HI = lax.Precision.HIGHEST
CDEG = 8
CELLS = 32 * 256 * 1024
LEVELS = ((8, 32, 128), (4, 16, 64), (2, 8, 32))
TOP = 8
DEEP_ROWS = {1: 48, 2: 40}
OWN1, OWN2 = pl.ds(16, 16), pl.ds(16, 8)


def cheb_constants(low, high, degree):
    middle, spread = 0.5 * (high + low), 0.5 * (high - low)
    factor = middle / spread
    old = 1.0 / factor
    steps = []
    for _ in range(degree - 1):
        new = 1.0 / (2.0 * factor - old)
        steps.append((new * old, 2.0 * new / spread))
        old = new
    return 1.0 / middle, steps


FIRST, STEPS = cheb_constants(0.5, 2.0, 3)
COARSE_FIRST, COARSE_STEPS = cheb_constants(0.1, 2.0, CDEG)


def lanes_of(shape):
    return lax.broadcasted_iota(jnp.int32, shape, len(shape) - 1)


def rows_of(shape):
    return lax.broadcasted_iota(jnp.int32, shape, len(shape) - 2)


def block(x, rows):
    return pl.ds(pl.multiple_of(x * rows, 8), rows)


def kernel(
    forcing, pressure, viscosity, forward, owner,
    adjoint, pnext, gradient,
    load, base, fwd, base_z, fwd_z,
    buf0, zbuf, faces0, faces1, faces2, links0, diag0, inv0, res0, sol0, rim0, hbuf, hz, applied,
    coef1, coef2, inv1, inv2, right1, left1, right2, deep1, deep2, sol1, sol2,
    zsend1, zgot1, dense2, dgot2,
    tmp, flat, erows, tile, got1, got2, got3,
    in_sem, send_sem, recv_sem, fsend, frecv, send1, recv1, send2, recv2, send3, recv3,
    dsend1, drecv1, dsend2, drecv2, hsend, hrecv,
):
    me = tuple(lax.axis_index(a) for a in AXES)
    rad, lat, lon = me

    def device(*steps):
        return tuple(
            lax.rem(m + (s % n), n) if s % n else m for m, s, n in zip(me, steps, SIZES)
        )

    up = [device(1, 0, 0), device(0, 1, 0), device(0, 0, 1)]
    down = [device(-1, 0, 0), device(0, -1, 0), device(0, 0, -1)]
    along = [device(0, 0, k) for k in range(1, 8)]
    across = [device(0, k, 0) for k in range(1, 8)]
    through = [device(k, 0, 0) for k in range(1, 4)]
    near1 = [
        (a, b, c) for a in (0, 1, -1) for b in (0, 1, -1) for c in (0, 1, -1) if a or b or c
    ]
    near2 = [
        (a, b, c) for a in range(4) for b in (0, 1, -1) for c in (0, 1, -1) if a or b or c
    ]
    peers = [device(*o) for o in near2] + along[1:6] + across[1:6]

    own_rows = pl.ds(TOP, 32)
    loads = [
        pltpu.make_async_copy(viscosity, base.at[0, pl.ds(1, 8), own_rows], in_sem.at[0]),
        pltpu.make_async_copy(pressure, base.at[1, pl.ds(1, 8), own_rows], in_sem.at[1]),
        pltpu.make_async_copy(forcing, load, in_sem.at[2]),
        pltpu.make_async_copy(forward, fwd.at[:, pl.ds(1, 8), own_rows], in_sem.at[3]),
    ]
    for copy in loads:
        copy.start()

    def clear(ref, *at):
        ref[at] = jnp.zeros(ref[at].shape, F32)

    every, low_rows, high_rows = slice(None), slice(8, 16), slice(32, 40)
    for plane in (0, 9):
        clear(buf0, every, every, plane, slice(8, 40))
        clear(base, every, plane, slice(8, 40))
        clear(fwd, every, plane, slice(8, 40))
        clear(hbuf, every, plane, slice(8, 40))
    clear(coef1, every, slice(0, 12), low_rows)
    clear(coef1, every, slice(0, 12), slice(32, 48))
    for planes in (slice(0, 4), slice(8, 12)):
        clear(coef1, every, planes, slice(16, 32))
        clear(right1, every, planes, slice(16, 32))
        clear(left1, every, planes, slice(16, 32))
    for ref in (right1, left1):
        clear(ref, every, every, low_rows)
        clear(ref, every, every, high_rows)
    clear(deep1, every, every, every, slice(0, 8))
    clear(deep1, every, every, every, slice(40, 48))
    clear(deep2, every, every, every, slice(0, 8))
    clear(deep2, every, every, every, slice(32, 40))
    for plane in (1, 10):
        clear(coef2, every, plane)
        clear(deep2, every, every, plane)
    clear(coef2, every, every, slice(32, 40))
    for plane in (0, 1, 10, 11):
        clear(sol2, every, plane, slice(8, 32))
    for side in (0, 2):
        clear(zgot1, every, side)

    barrier = pltpu.get_barrier_semaphore()
    for target in peers:
        pl.semaphore_signal(barrier, inc=1, device_id=target, device_id_type=MESH)

    def remote(src, dst, ssem, rsem, target):
        return pltpu.make_async_remote_copy(
            src_ref=src, dst_ref=dst, send_sem=ssem, recv_sem=rsem,
            device_id=target, device_id_type=MESH,
        )

    lane8 = lanes_of((8, 128))

    zero8 = jnp.zeros((8, 128), F32)

    def pack(accs, planes, x, lows=True, highs=True):
        parts = [p[8 * g : 8 * g + 8] for p in planes for g in range(4)]
        n = len(parts)
        low = high = zero8
        for j, part in enumerate(parts):
            turned = pltpu.roll(part, j, 1) if j else part
            if lows:
                low = jnp.where(lane8 == j, turned, low)
            if highs:
                high = jnp.where(lane8 == (127 + j) % 128, turned, high)
        return (
            accs[0] + pltpu.roll(low, n * x, 1) if lows else accs[0],
            accs[1] + pltpu.roll(high, n * x, 1) if highs else accs[1],
        )

    def merged(before, after):
        before, after = pltpu.roll(before, 1, 1), pltpu.roll(after, 127, 1)
        even = jnp.bitwise_and(lane8, 1) == 0
        return jnp.where(even, before, after), jnp.where(even, after, before)

    def rims_of(halo, n, x):
        turn_back = lax.rem(128 - n * x, 128)
        halo = [pltpu.roll(h, turn_back, 1) for h in halo]
        return [pltpu.roll(halo[j % 2], 128 - j, 1) if j else halo[0] for j in range(n)]

    lane32, lane16 = lanes_of((32, 128)), lanes_of((16, 128))

    def shifted(v, rims):
        rim = jnp.concatenate(rims, 0) if isinstance(rims, list) else rims
        low = jnp.where(lane32 == 0, rim, pltpu.roll(v, 1, 1))
        high = jnp.where(lane32 == 127, rim, pltpu.roll(v, 127, 1))
        return low, high

    def guarded(copy, step):
        sends_it, gets_it = (rad < 3, rad > 0) if step == 1 else (rad > 0, rad < 3)

        def start():
            pl.when(sends_it)(copy.start)

        def wait():
            pl.when(sends_it)(copy.wait_send)
            pl.when(gets_it)(copy.wait_recv)

        return start, wait

    def plain(copy):
        return copy.start, copy.wait

    def sends(buf, zref, ssem, rsem):
        rows, planes = pl.ds(TOP, 32), pl.ds(1, 8)
        parts = [
            (buf.at[:, 8, rows], buf.at[:, 0, rows], up[0]),
            (buf.at[:, 1, rows], buf.at[:, 9, rows], down[0]),
            (buf.at[:, planes, pl.ds(TOP + 31, 1)], buf.at[:, planes, pl.ds(TOP - 1, 1)], up[1]),
            (buf.at[:, planes, pl.ds(TOP, 1)], buf.at[:, planes, pl.ds(TOP + 32, 1)], down[1]),
            (zref.at[1], zref.at[2], up[2]),
            (zref.at[0], zref.at[3], down[2]),
        ]
        copies = [
            remote(src, dst, ssem.at[i], rsem.at[i], target)
            for i, (src, dst, target) in enumerate(parts)
        ]
        return [guarded(copies[0], 1), guarded(copies[1], -1)] + [plain(copy) for copy in copies[2:]]

    turn = [0]

    def send_all(accs, buf, zref, ssem, rsem):
        zref[0], zref[1] = accs
        copies = sends(buf, zref, ssem, rsem)
        for start, _ in copies:
            start()

        def finish():
            for _, wait in copies:
                wait()
            return merged(zref[2], zref[3])

        return finish

    def exchange(accs, buf=None):
        p = turn[0] % 2
        turn[0] += 1
        return send_all(accs, buf0.at[p] if buf is None else buf, zbuf.at[p], send_sem.at[p], recv_sem.at[p])

    for copy in loads[:2]:
        copy.wait()

    def pack_base(x, accs):
        return pack(accs, [base[c, x + 1, own_rows, :] for c in range(2)], x)

    accs = lax.fori_loop(0, 8, pack_base, (zero8, zero8), unroll=2)
    pl.semaphore_wait(barrier, len(peers))
    finish = exchange(accs, base)
    loads[3].wait()

    def pack_fwd(x, accs):
        return pack(accs, [fwd[c, x + 1, own_rows, :] for c in range(3)], x, highs=False)

    fwd_z[0] = lax.fori_loop(0, 8, pack_fwd, (zero8, zero8), unroll=2)[0]
    fwd_parts = [
        (fwd.at[:, 1, own_rows], fwd.at[:, 9, own_rows], down[0]),
        (fwd.at[:, pl.ds(1, 8), pl.ds(TOP, 1)], fwd.at[:, pl.ds(1, 8), pl.ds(TOP + 32, 1)], down[1]),
        (fwd_z.at[0], fwd_z.at[1], down[2]),
    ]
    fwd_copies = [
        remote(src, dst, fsend.at[i], frecv.at[i], target)
        for i, (src, dst, target) in enumerate(fwd_parts)
    ]
    fwd_copies = [guarded(fwd_copies[0], -1)] + [plain(copy) for copy in fwd_copies[1:]]
    for begin, _ in fwd_copies:
        begin()

    grid_row, grid_lane = rows_of((128, 128)), lanes_of((128, 128))
    pair = (grid_row // 2 == grid_lane).astype(F32)
    own_pair = jnp.where(grid_row < 64, pair, 0.0)
    pick = [(grid_row == 2 * grid_lane + s).astype(F32) for s in range(2)]
    spread0 = (grid_row == grid_lane // 2).astype(F32)
    spread1 = (grid_row == jnp.where(grid_lane < 96, 0, 64) + grid_lane // 2).astype(F32)

    def times(a, b):
        return jnp.dot(a, b, precision=HI, preferred_element_type=F32)

    def edge(x, side, nx):
        at_edge = (rad == 0) & (x == 0) if side == 0 else (rad == 3) & (x == nx - 1)
        return jnp.where(at_edge, 0.0, 1.0).astype(F32)

    def edge_rows(side, ny):
        row = rows_of((ny, 128))
        at_edge = (lat == 0) & (row == 0) if side == 0 else (lat == 7) & (row == ny - 1)
        return jnp.where(at_edge, 0.0, 1.0).astype(F32)

    loads[2].wait()
    halo = finish()

    def setup_plane(x, accs):
        v = base[0, x + 1, own_rows, :]
        rims = rims_of(halo, 8, x)
        low_z, high_z = shifted(v, rims[:4])
        lower_x, upper_x, lower_y, upper_y = edge(x, 0, 8), edge(x, 1, 8), edge_rows(0, 32), edge_rows(1, 32)
        six = [
            0.5 * (v + lower_x * base[0, x, own_rows, :]),
            0.5 * (v + upper_x * base[0, x + 2, own_rows, :]),
            0.5 * (v + lower_y * base[0, x + 1, pl.ds(TOP - 1, 32), :]),
            0.5 * (v + upper_y * base[0, x + 1, pl.ds(TOP + 1, 32), :]),
            0.5 * (v + low_z),
            0.5 * (v + high_z),
        ]
        at = block(x, 32)
        for k in range(6):
            faces0[k, at, :] = six[k]
        masks = (lower_x, upper_x, lower_y, upper_y)
        for k in range(6):
            links0[k, at, :] = six[k] * masks[k] if k < 4 else six[k]
        diag = six[0] + six[1] + six[2] + six[3] + six[4] + six[5]
        inv = 1.0 / diag
        diag0[at, :] = diag
        inv0[at, :] = inv
        p = base[1, x + 1, own_rows, :]
        _, high_p = shifted(p, rims[4:])
        grads = [
            base[1, x + 2, own_rows, :] * upper_x - p,
            base[1, x + 1, pl.ds(TOP + 1, 32), :] * upper_y - p,
            high_p - p,
        ]
        updates = []
        for c in range(3):
            right = load[c, x] - grads[c]
            res0[c, at, :] = right
            update = inv * right * FIRST
            sol0[c, at, :] = update
            buf0[1, c, x + 1, own_rows, :] = update
            updates.append(update)
        return pack(accs, updates, x)

    start = lax.fori_loop(0, 8, setup_plane, (zero8, zero8))

    def coarsen(level, fine, coarse):
        nx, ny, _ = LEVELS[level]
        half_x, half_y = nx // 2, ny // 2
        n = half_x * half_y

        def one(x, carry):
            for k in range(6):
                way, side = k // 2, k % 2
                if way == 0:
                    plane = fine[k, block(2 * x + side, ny), :]
                else:
                    plane = fine[k, block(2 * x, ny), :] + fine[k, block(2 * x + 1, ny), :]
                tmp[k, pl.ds(0, ny), :] = plane
            for k in range(6):
                way, side = k // 2, k % 2
                if way == 1:
                    both = tmp[k, pl.ds(side, half_y, 2), :]
                else:
                    both = tmp[k, pl.ds(0, half_y, 2), :] + tmp[k, pl.ds(1, half_y, 2), :]
                flat[k, block(x, half_y), :] = both
            return carry

        lax.fori_loop(0, half_x, one, 0)
        sums = times(flat[0:4, :n, :].reshape(4 * n, 128), pair).reshape(4, n, 128)
        for k in range(4):
            coarse[k] = sums[k]
        for k in range(4, 6):
            coarse[k] = times(flat[k, :n, :], pick[k - 4])

    def coefficients(level, faces, x):
        nx, ny, _ = LEVELS[level]
        six = [faces[k, pl.ds(x * ny, ny), :] for k in range(6)]
        total = six[0] + six[1] + six[2] + six[3] + six[4] + six[5]
        return [total, six[0] * edge(x, 0, nx), six[2] * edge_rows(0, ny), six[4]]

    def invert(coef, inv, planes):
        def one(x, carry):
            d = coef[0, x]
            inv[x] = jnp.where(d > 0.0, 1.0 / jnp.where(d > 0.0, d, 1.0), 0.0)
            return carry

        lax.fori_loop(0, planes, one, 0)

    side_lanes = (lane8 < 68) | (lane8 >= 124)

    def exchange1(use, ref, depth_up, depth_down):
        n = ref.shape[0]
        zlow = zhigh = zero8
        for x in range(4):
            for a in range(n):
                for g in range(2):
                    at = 4 * ((x * n + a) * 2 + g)
                    part = ref[a, 4 + x, pl.ds(16 + 8 * g, 8), :]
                    turned = pltpu.roll(part, at, 1) if at else part
                    zlow = jnp.where((lane8 >= at) & (lane8 < at + 4), turned, zlow)
                    top = (60 + at) % 128
                    zhigh = jnp.where((lane8 >= top) & (lane8 < top + 4), turned, zhigh)
        zsend1[use, 0] = zlow
        zsend1[use, 1] = zhigh
        copies = []
        for i, (a, b, c) in enumerate(near1):
            if c:
                src = zsend1.at[use, (c + 1) // 2]
                dst = zgot1.at[use, 1 - a, 1 - b, (1 - c) // 2]
            else:
                from_x, to_x, from_y, to_y = pl.ds(4, 4), pl.ds(4, 4), OWN1, OWN1
                if a == 1:
                    from_x, to_x = pl.ds(8 - depth_up, depth_up), pl.ds(4 - depth_up, depth_up)
                if a == -1:
                    from_x, to_x = pl.ds(4, depth_down), pl.ds(8, depth_down)
                if b == 1:
                    from_y, to_y = pl.ds(28, 4), pl.ds(12, 4)
                if b == -1:
                    from_y, to_y = pl.ds(16, 4), pl.ds(32, 4)
                src, dst = ref.at[:, from_x, from_y], ref.at[:, to_x, to_y]
            copy = remote(src, dst, dsend1.at[use, i], drecv1.at[use, i], device(a, b, c))
            copies.append((a, copy))

        def each(way, do):
            group = [copy for a, copy in copies if a == way]
            for copy in group:
                do(copy)

        for way, there in ((1, rad < 3), (-1, rad > 0)):
            pl.when(there)(lambda way=way: each(way, lambda copy: copy.start()))
        each(0, lambda copy: copy.start())

        def finish(low_plane, high_plane):
            for way, sends_it, gets_it in ((1, rad < 3, rad > 0), (-1, rad > 0, rad < 3)):
                pl.when(sends_it)(lambda way=way: each(way, lambda copy: copy.wait_send()))
                pl.when(gets_it)(lambda way=way: each(way, lambda copy: copy.wait_recv()))
            each(0, lambda copy: copy.wait())

            def one(plane, carry):
                dx, x = lax.div(plane, 4), lax.rem(plane, 4)
                back = lax.rem(192 - 8 * n * x, 128)
                for dy, groups in ((0, (1,)), (1, (2, 3)), (2, (4,))):
                    above = pltpu.roll(zgot1[use, dx, dy, 1], back, 1)
                    below = pltpu.roll(zgot1[use, dx, dy, 0], back, 1)
                    both = jnp.where((lane8 >= 64) & (lane8 < 96), above, below)
                    for a in range(n):
                        for group in groups:
                            g = (1, group - 2, 0)[dy]
                            at = (128 - 4 * (2 * a + g)) % 128
                            side = pltpu.roll(both, at, 1) if at else both
                            rows = pl.ds(8 * group, 8)
                            own = ref[a, plane, rows, :]
                            side = jnp.where(side_lanes, side, 0.0)
                            ref[a, plane, rows, :] = jnp.where(lane8 < 64, own, side)
                return carry

            lax.fori_loop(low_plane, high_plane, one, 0)

        return finish

    def exchange2(use, tiles):
        n = len(tiles)
        for i, t in enumerate(tiles):
            dense2[use, i] = t
            dgot2[use, rad, 1, 1, i] = t
        copies = []
        for i, (a, b, c) in enumerate(near2):
            src = dense2.at[use, pl.ds(0, n)]
            dst = dgot2.at[use, rad, 1 - b, 1 - c, pl.ds(0, n)]
            copies.append(remote(src, dst, dsend2.at[use, i], drecv2.at[use, i], device(a, b, c)))
        for copy in copies:
            copy.start()

        def finish():
            for copy in copies:
                copy.wait()

        return finish

    def packed2(parts):
        tiles = []
        for i in range(0, len(parts), 4):
            out = zero8
            for j, part in enumerate(parts[i : i + 4]):
                part = pltpu.roll(part, 32 * j, 1) if j else part
                out = jnp.where((lane8 >= 32 * j) & (lane8 < 32 * j + 32), part, out)
            tiles.append(out)
        return tiles

    def turned2(use, source, dy, dz, tile_at, lanes):
        t = dgot2[use, source, dy, dz, tile_at]
        return pltpu.roll(t, lanes % 128, 1) if lanes % 128 else t

    def joined2(use, source, dy, part):
        i, at = part // 4, 32 * (part % 4)
        own = turned2(use, source, dy, 1, i, -at)
        after = turned2(use, source, dy, 2, i, 32 - at)
        before = turned2(use, source, dy, 0, i, 96 - at)
        out = jnp.where(lane8 < 32, own, jnp.where(lane8 < 64, after, before))
        return jnp.where((lane8 < 64) | (lane8 >= 96), out, 0.0)

    def unpack2(use, ref):
        n = ref.shape[0]

        def one(source, carry):
            for a in range(n):
                for x in range(2):
                    for dy in range(3):
                        ref[a, 2 + 2 * source + x, pl.ds(8 + 8 * dy, 8), :] = joined2(use, source, dy, 2 * a + x)
            return carry

        lax.fori_loop(0, 4, one, 0)

    coefs, invs = (None, coef1, coef2), (None, inv1, inv2)
    deeps, sols = (None, deep1, deep2), (None, sol1, sol2)

    def begin_deep(level, res, planes, keep):
        rows = pl.ds(8, DEEP_ROWS[level] - 16)

        def one(x, carry):
            for c in range(3):
                update = FIRST * invs[level][x, rows, :] * res[c, x, rows, :]
                deeps[level][0, c, x, rows, :] = update
                sols[level][c, x, rows, :] = update
            return carry

        lax.fori_loop(planes[0], planes[1], one, 0, unroll=2)

    def sweep_deep(level, p, res, out, planes, step, initial=False, rows=None):
        coef, inv, deep, sol = coefs[level], invs[level], deeps[level], sols[level]
        first, count = (8, DEEP_ROWS[level] - 16) if rows is None else rows
        here, under, over = pl.ds(first, count), pl.ds(first - 1, count), pl.ds(first + 1, count)

        def one(x, carry):
            diag, lower_x, upper_x = coef[0, x, here, :], coef[1, x, here, :], coef[1, x + 1, here, :]
            lower_y, upper_y, lower_z = coef[2, x, here, :], coef[2, x, over, :], coef[3, x, here, :]
            upper_z = pltpu.roll(lower_z, 127, 1)
            for c in range(3):
                v = deep[p, c, x, here, :]
                total = diag * v - lower_x * deep[p, c, x - 1, here, :] - upper_x * deep[p, c, x + 1, here, :]
                total = total - lower_y * deep[p, c, x, under, :] - upper_y * deep[p, c, x, over, :]
                total = total - lower_z * pltpu.roll(v, 1, 1) - upper_z * pltpu.roll(v, 127, 1)
                r = res[c, x, here, :] - total
                out[c, x, here, :] = r
                if step is None:
                    continue
                if initial:
                    update = FIRST * inv[x, here, :] * r
                    sol[c, x, here, :] = sol[c, x, here, :] + v + update
                else:
                    update = step[0] * v + step[1] * inv[x, here, :] * r
                    sol[c, x, here, :] = sol[c, x, here, :] + update
                deep[1 - p, c, x, here, :] = update
            return carry

        lax.fori_loop(planes[0], planes[1], one, 0, unroll=2)

    def sweep(p, halo, step, initial=False, emit=None):
        def plane(x, accs):
            at = block(x, 32)
            diag, inv = diag0[at, :], inv0[at, :]
            ls = [links0[k, at, :] for k in range(6)]
            rims = rims_of(halo, 12, x) if halo is not None else None
            packs = []
            for c in range(3):
                v = buf0[p, c, x + 1, own_rows, :]
                low_z, high_z = shifted(v, rims[4 * c : 4 * c + 4] if rims else rim0[c, x])
                total = diag * v - ls[0] * buf0[p, c, x, own_rows, :]
                total = total - ls[1] * buf0[p, c, x + 2, own_rows, :]
                total = total - ls[2] * buf0[p, c, x + 1, pl.ds(TOP - 1, 32), :]
                total = total - ls[3] * buf0[p, c, x + 1, pl.ds(TOP + 1, 32), :]
                total = total - ls[4] * low_z - ls[5] * high_z
                r = res0[c, at, :] - total
                if step is None:
                    res0[c, at, :] = r
                    continue
                if initial:
                    update = FIRST * inv * r
                    after = sol0[c, at, :] + v + update
                else:
                    update = step[0] * v + step[1] * inv * r
                    after = sol0[c, at, :] + update
                if emit is None:
                    sol0[c, at, :] = after
                    res0[c, at, :] = r
                    buf0[1 - p, c, x + 1, own_rows, :] = update
                    packs.append(update)
                else:
                    packs.append(after)
            if step is None:
                return accs
            low, high = pack(accs, packs, x)
            if emit is not None:
                emit(packs, x)
            return low, high

        return lax.fori_loop(0, 8, plane, (zero8, zero8), unroll=2)

    def restrict(source, rows, level, matrix):
        nx, ny, _ = LEVELS[level]
        half_x, half_y = nx // 2, ny // 2
        n = half_x * half_y

        def one(x, carry):
            for c in range(3):
                tmp[c, pl.ds(0, ny), :] = source(c, 2 * x) + source(c, 2 * x + 1)
            for c in range(3):
                flat[c, block(x, half_y), :] = tmp[c, pl.ds(0, half_y, 2), :] + tmp[c, pl.ds(1, half_y, 2), :]
            return carry

        lax.fori_loop(0, half_x, one, 0)
        return times(flat[0:3, :n, :].reshape(3 * n, 128), matrix)

    def gather(use):
        first = [
            remote(tile.at[use, 0], got1.at[use, lon], send1.at[use, i], recv1.at[use, i], target)
            for i, target in enumerate(along)
        ]
        second = [
            remote(tile.at[use, 1], got2.at[use, block(lat, 8)], send2.at[use, i], recv2.at[use, i], target)
            for i, target in enumerate(across)
        ]

        def begin(value):
            tile[use, 0] = value
            got1[use, lon] = value
            for copy in first:
                copy.start()

        def middle():
            for copy in first:
                copy.wait()
            total = got1[use, 0]
            for k in range(1, 8):
                total = total + got1[use, k]
            tile[use, 1] = total
            got2[use, block(lat, 8), :] = total
            for copy in second:
                copy.start()

        def end():
            for copy in second:
                copy.wait()

        return begin, middle, end

    lane1 = lanes_of((1, 128))
    runs = jnp.bitwise_and(owner[0, 0:1, :], 31)
    runs = jnp.concatenate([runs, jnp.full((1, 96), -1, jnp.int32)], 1)

    def member_of(columns):
        return (grid_row == jnp.broadcast_to(columns, (128, 128))).astype(F32)

    own_member = member_of(runs)

    def to_runs(rows):
        return lax.dot_general(
            rows, own_member, (((1,), (1,)), ((), ())), precision=HI, preferred_element_type=F32
        )

    def stacked(rows, count=8):
        out = jnp.zeros((count, 128), F32)
        at = rows_of((count, 128))
        for i, row in enumerate(rows):
            out = jnp.where(at == i, jnp.broadcast_to(row, (count, 128)), out)
        return out

    def rowsum(plane):
        return jnp.sum(plane, axis=0, keepdims=True)

    def run_sides():
        f = faces2
        wide = jnp.broadcast_to(runs, (8, 128))
        first_cell = (lane1 == 0) | (runs != pltpu.roll(wide, 1, 1)[0:1])
        last_cell = (lane1 == 31) | (runs != pltpu.roll(wide, 127, 1)[0:1])
        sides = [
            rowsum(f[0, 0:8, :]),
            rowsum(f[1, 8:16, :]),
            f[2, 0:1, :] + f[2, 8:9, :],
            f[3, 7:8, :] + f[3, 15:16, :],
            jnp.where(first_cell, rowsum(f[4, 0:8, :] + f[4, 8:16, :]), 0.0),
            jnp.where(last_cell, rowsum(f[5, 0:8, :] + f[5, 8:16, :]), 0.0),
        ]
        whole = sides[0] + sides[1] + sides[2] + sides[3] + sides[4] + sides[5]
        return to_runs(stacked([sides[0], sides[2], sides[4], whole]))

    def coarse_solve(meanwhile):
        begin, middle, end = gather(0)
        rows = []
        for block_x in range(4):
            for c in range(3):
                both = right2[c, 2 + 2 * block_x, OWN2, :] + right2[c, 3 + 2 * block_x, OWN2, :]
                rows.append(rowsum(both))
        sums = to_runs(stacked(rows, 16))
        row8 = rows_of((8, 128))
        value = zero8
        for block_x in range(4):
            part = jnp.where(row8 < 3, 0.0, pltpu.roll(dgot2[0, block_x, 1, 1, 2], 2, 0))
            for c in range(3):
                row = jnp.broadcast_to(sums[3 * block_x + c : 3 * block_x + c + 1], (8, 128))
                part = jnp.where(row8 == c, row, part)
            value = value + (pltpu.roll(part, 32 * block_x, 1) if block_x else part)
        begin(value)
        meanwhile()
        middle()
        end()

        def all_of(i):
            return got2[0, pl.ds(i, 8, 8), :]

        wrap = jnp.bitwise_and(lane8, 31)

        def lower_z(v):
            return jnp.where(wrap == 0, pltpu.roll(v, 97, 1), pltpu.roll(v, 1, 1))

        def upper_z(v):
            return jnp.where(wrap == 31, pltpu.roll(v, 31, 1), pltpu.roll(v, 127, 1))

        link_x = jnp.where(lane8 < 32, 0.0, all_of(3))
        link_y = jnp.where(row8 == 0, 0.0, all_of(4))
        link_z = all_of(5)
        link_xu, link_yu, link_zu = pltpu.roll(link_x, 96, 1), pltpu.roll(link_y, 7, 0), upper_z(link_z)
        diagonal = all_of(6)
        inverse = 1.0 / diagonal

        def operate(v):
            out = diagonal * v - link_x * pltpu.roll(v, 32, 1) - link_xu * pltpu.roll(v, 96, 1)
            out = out - link_y * pltpu.roll(v, 1, 0) - link_yu * pltpu.roll(v, 7, 0)
            return out - link_z * lower_z(v) - link_zu * upper_z(v)

        rs = [all_of(c) for c in range(3)]
        ds = [inverse * r * COARSE_FIRST for r in rs]
        es = list(ds)
        for a, b in COARSE_STEPS:
            rs = [r - operate(d) for r, d in zip(rs, ds)]
            ds = [a * d + b * inverse * r for r, d in zip(rs, ds)]
            es = [e + d for e, d in zip(es, ds)]
        for c in range(3):
            erows[c] = es[c]
        lats = [lax.rem(lat + 7, 8), lat, lax.rem(lat + 1, 8)]
        rows = [erows[c, pl.ds(at, 1), :] for c in range(3) for at in lats]
        rows = stacked(rows, 16)
        rows = [rows if k == 0 else pltpu.roll(rows, 128 - 32 * k, 1) for k in range(4)]
        spans = times(jnp.concatenate(rows, 0), region_member())
        for block_x in range(4):
            for c in range(3):
                for dy in range(3):
                    i = 16 * block_x + 3 * c + dy
                    row = jnp.broadcast_to(spans[i : i + 1], (8, 128))
                    for x in range(2):
                        deep2[1, c, 2 + 2 * block_x + x, pl.ds(8 + 8 * dy, 8), :] = row

    def region_member():
        own, before, after = (turned2(0, rad, 1, k, 2, t)[0:1] for k, t in ((1, 0), (0, 96), (2, 32)))
        columns = jnp.where(lane1 < 32, own, jnp.where(lane1 < 64, after, before))
        columns = jnp.where((lane1 < 64) | (lane1 >= 96), columns, -1.0).astype(jnp.int32)
        return member_of(columns)

    pending = {}

    def while_first():
        coarsen(0, faces0, faces1)
        for x in range(4):
            for k, value in enumerate(coefficients(1, faces1, x)):
                coef1[k, 4 + x, OWN1, :] = value
        pending["coef1"] = exchange1(0, coef1, 3, 4)

    def while_second():
        coarsen(1, faces1, faces2)
        values = [coefficients(2, faces2, x) for x in range(2)]
        last = jnp.where(rows_of((8, 128)) == 0, runs.astype(F32), pltpu.roll(run_sides(), 1, 0))
        parts = packed2([values[x][k] for k in range(4) for x in range(2)])
        pending["coef2"] = exchange2(0, parts + [last])

        def weigh(x, accs):
            v, inv = base[0, x + 1, own_rows, :], inv0[block(x, 32), :]
            parts = [2.0 * inv * (v - faces0[2 * c + 1, block(x, 32), :]) for c in range(3)]
            for c in range(3):
                hbuf[c, x + 1, own_rows, :] = parts[c]
            return pack(accs, parts, x)

        accs = lax.fori_loop(0, 8, weigh, (zero8, zero8), unroll=2)
        pending["h"] = send_all(accs, hbuf, hz, hsend, hrecv)

    def apply_to_h():
        halo = pending["h"]()

        def one(x, carry):
            at = block(x, 32)
            rims = rims_of(halo, 12, x)
            for c in range(3):
                v = hbuf[c, x + 1, own_rows, :]
                low_z, high_z = shifted(v, rims[4 * c : 4 * c + 4])
                total = diag0[at, :] * v - links0[0, at, :] * hbuf[c, x, own_rows, :]
                total = total - links0[1, at, :] * hbuf[c, x + 2, own_rows, :]
                total = total - links0[2, at, :] * hbuf[c, x + 1, pl.ds(TOP - 1, 32), :]
                total = total - links0[3, at, :] * hbuf[c, x + 1, pl.ds(TOP + 1, 32), :]
                applied[c, at, :] = total - links0[4, at, :] * low_z - links0[5, at, :] * high_z
            return carry

        lax.fori_loop(0, 8, one, 0, unroll=2)

    def while_third():
        pending["coef1"](0, 12)
        invert(coef1, inv1, 12)

    accs = start
    for step, meanwhile in ((STEPS[0], while_first), (STEPS[1], while_second), (None, while_third)):
        p = turn[0] % 2
        finish = exchange(accs)
        meanwhile()
        accs = sweep(p, finish(), step)

    sums = restrict(lambda c, x: res0[c, block(x, 32), :], 32, 0, pair)
    for c in range(3):
        for x in range(4):
            right1[c, 4 + x, OWN1, :] = sums[64 * c + 16 * x : 64 * c + 16 * x + 16]
    finish = exchange1(1, right1, 3, 3)
    pending["coef2"]()
    unpack2(0, coef2)
    invert(coef2, inv2, 12)
    finish(1, 11)
    begin_deep(1, right1, (1, 11), None)
    sweep_deep(1, 0, right1, right1, (2, 10), STEPS[0])
    sweep_deep(1, 1, right1, right1, (3, 9), STEPS[1])
    sweep_deep(1, 0, right1, left1, (4, 8), None, rows=(16, 16))

    sums = restrict(lambda c, x: left1[c, 4 + x, OWN1, :], 16, 1, own_pair)
    finish2 = exchange2(1, packed2([sums[16 * c + 8 * x : 16 * c + 8 * x + 8] for c in range(3) for x in range(2)]))
    finish1 = exchange1(2, left1, 3, 3)
    apply_to_h()
    finish2()
    unpack2(1, right2)
    all2 = (2, 10)
    begin_deep(2, right2, all2, None)
    sweep_deep(2, 0, right2, right2, all2, STEPS[0])
    sweep_deep(2, 1, right2, right2, all2, STEPS[1])
    sweep_deep(2, 0, right2, right2, all2, None)
    coarse_solve(lambda: finish1(1, 11))
    sweep_deep(2, 1, right2, right2, all2, STEPS[0], initial=True)
    sweep_deep(2, 0, right2, right2, all2, STEPS[0])
    sweep_deep(2, 1, right2, right2, all2, STEPS[1])

    def gather_rows(k, carry):
        for c in range(3):
            flat[c, block(k, 16), :] = sol2[c, 2 * rad + k, pl.ds(12, 16), :]
        return carry

    lax.fori_loop(0, 6, gather_rows, 0)
    for c in range(3):
        flat[c, 0:96, :] = times(flat[c, 0:96, :], spread1)

    def to_level1(k, carry):
        for c in range(3):
            value = flat[c, block(k, 16), :]
            for s in range(2):
                for t in range(2):
                    deep1[1, c, 2 * k + s, pl.ds(8 + t, 16, 2), :] = value
        return carry

    lax.fori_loop(0, 6, to_level1, 0)
    sweep_deep(1, 1, left1, left1, (1, 11), STEPS[0], initial=True)
    sweep_deep(1, 0, left1, left1, (2, 10), STEPS[0])
    sweep_deep(1, 1, left1, left1, (3, 9), STEPS[1])

    p = turn[0] % 2
    turn[0] += 1
    for c in range(3):
        flat[c] = times(sol1[c, 3:9, 12:36, :].reshape(144, 128), spread0)

    for k in range(6):
        for c in range(3):
            value = flat[c, 24 * k : 24 * k + 24, :]
            tmp[c, pl.ds(0, 24, 2), :] = value
            tmp[c, pl.ds(1, 24, 2), :] = value
            if 1 <= k <= 4:
                coarse = sol1[c, 3 + k, OWN1, :]
                rim = jnp.where(lane16 == 0, pltpu.roll(coarse, 1, 1), pltpu.roll(coarse, 63, 1))
                tmp[3 + c, pl.ds(0, 16, 2), :] = rim
                tmp[3 + c, pl.ds(1, 16, 2), :] = rim
        for c in range(3):
            for at in (2 * k - 1, 2 * k):
                if 0 <= at <= 9:
                    buf0[p, c, at] = tmp[c, pl.ds(0, 48), :]
                if 1 <= at <= 8:
                    rim0[c, at - 1] = tmp[3 + c, pl.ds(0, 32), :]

    accs = sweep(p, None, STEPS[0], initial=True)
    p = turn[0] % 2
    accs = sweep(p, exchange(accs)(), STEPS[0])
    p = turn[0] % 2
    finish = exchange(accs)
    begin, middle, end = gather(1)

    def add_up(x, total):
        at = block(x, 32)
        v = base[0, x + 1, own_rows, :]
        part = base[1, x + 1, own_rows, :]
        for c in range(3):
            update = buf0[p, c, x + 1, own_rows, :]
            weight = 2.0 * (v - faces0[2 * c + 1, at, :])
            h = hbuf[c, x + 1, own_rows, :]
            part = part - weight * (sol0[c, at, :] + STEPS[1][0] * update)
            part = part - STEPS[1][1] * (h * res0[c, at, :] - applied[c, at, :] * update)
        return total + (part[0:8] + part[8:16] + part[16:24] + part[24:32])

    begin(lax.fori_loop(0, 8, add_up, zero8, unroll=2))
    final = 1 - p

    def emit(afters, x):
        for c, after in enumerate(afters):
            adjoint[c, x] = after
            buf0[final, c, x + 1, own_rows, :] = after

    accs = sweep(p, finish(), STEPS[1], emit=emit)

    finish = exchange(accs)
    for _, wait in fwd_copies:
        wait()
    middle()
    halo = finish()
    fwd_halo = merged(zero8, fwd_z[1])

    def outputs(x, carry):
        v = base[0, x + 1, own_rows, :]
        keep_x, keep_y = edge(x, 1, 8), edge_rows(1, 32)
        ga, gf = [], []
        us = []
        rims, fwd_rims = rims_of(halo, 12, x), rims_of(fwd_halo, 12, x)
        for c in range(3):
            u = buf0[final, c, x + 1, own_rows, :]
            low_z, high_z = shifted(u, rims[4 * c : 4 * c + 4])
            ga.append([
                buf0[final, c, x + 2, own_rows, :] * keep_x - u,
                buf0[final, c, x + 1, pl.ds(TOP + 1, 32), :] * keep_y - u,
                high_z - u,
            ])
            us.append((u, low_z))
            w = fwd[c, x + 1, own_rows, :]
            _, high_w = shifted(w, fwd_rims[4 * c : 4 * c + 4])
            gf.append([
                fwd[c, x + 2, own_rows, :] * keep_x - w,
                fwd[c, x + 1, pl.ds(TOP + 1, 32), :] * keep_y - w,
                high_w - w,
            ])
        divergence = (
            us[0][0] - edge(x, 0, 8) * buf0[final, 0, x, own_rows, :]
            + (us[1][0] - edge_rows(0, 32) * buf0[final, 1, x + 1, pl.ds(TOP - 1, 32), :])
            + (us[2][0] - us[2][1])
        )
        pnext[x] = base[1, x + 1, own_rows, :] - v * divergence
        summed = gf[0][0] * ga[0][0] + gf[1][1] * ga[1][1] + gf[2][2] * ga[2][2]
        for d, e in ((0, 1), (0, 2), (1, 2)):
            summed = summed + 0.5 * (gf[e][d] + gf[d][e]) * (ga[e][d] + ga[d][e])
        gradient[x] = 2.0 * v * summed
        return carry

    end()
    total = zero8
    for b in range(8):
        total = total + got2[1, 8 * b : 8 * b + 8, :]
    tile[1, 2] = total
    got3[rad] = total
    last = [
        remote(tile.at[1, 2], got3.at[rad], send3.at[i], recv3.at[i], target)
        for i, target in enumerate(through)
    ]
    for copy in last:
        copy.start()
    lax.fori_loop(0, 8, outputs, 0, unroll=2)
    for copy in last:
        copy.wait()
    mean = jnp.sum(got3[0] + got3[1] + got3[2] + got3[3]) / CELLS

    def shift(x, carry):
        pnext[x] = pnext[x] - mean
        return carry

    lax.fori_loop(0, 8, shift, 0)


def per_device(forcing, pressure, viscosity, forward, owner):
    vmem, anywhere = pl.BlockSpec(memory_space=pltpu.VMEM), pl.BlockSpec(memory_space=pl.ANY)
    f32 = lambda *shape: pltpu.VMEM(shape, F32)
    dma = lambda *shape: pltpu.SemaphoreType.DMA(shape)
    return pl.pallas_call(
        kernel,
        out_shape=(
            jax.ShapeDtypeStruct((3, 8, 32, 128), F32),
            jax.ShapeDtypeStruct((8, 32, 128), F32),
            jax.ShapeDtypeStruct((8, 32, 128), F32),
        ),
        in_specs=[anywhere] * 4 + [vmem],
        out_specs=(vmem, vmem, vmem),
        scratch_shapes=[
            f32(3, 8, 32, 128), f32(2, 10, 48, 128), f32(3, 10, 48, 128), f32(1, 8, 128), f32(2, 8, 128),
            f32(2, 3, 10, 48, 128), f32(2, 4, 8, 128), f32(6, 256, 128), f32(6, 64, 128), f32(6, 16, 128),
            f32(6, 256, 128), f32(256, 128), f32(256, 128), f32(3, 256, 128), f32(3, 256, 128), f32(3, 8, 32, 128),
            f32(3, 10, 48, 128), f32(4, 8, 128), f32(3, 256, 128),
            f32(4, 13, 48, 128), f32(4, 12, 40, 128), f32(12, 48, 128), f32(12, 40, 128),
            f32(3, 12, 48, 128), f32(3, 12, 48, 128), f32(3, 12, 40, 128),
            f32(2, 3, 12, 48, 128), f32(2, 3, 12, 40, 128), f32(3, 12, 48, 128), f32(3, 12, 40, 128),
            f32(3, 2, 8, 128), f32(3, 3, 3, 2, 8, 128), f32(2, 3, 8, 128), f32(2, 4, 3, 3, 3, 8, 128),
            f32(6, 48, 128), f32(6, 144, 128), f32(3, 8, 128), f32(2, 3, 8, 128),
            f32(2, 8, 8, 128), f32(2, 64, 128), f32(4, 8, 128),
            dma(4), dma(2, 6), dma(2, 6), dma(3), dma(3), dma(2, 7), dma(2, 7), dma(2, 7), dma(2, 7), dma(3), dma(3),
            dma(3, 26), dma(3, 26), dma(2, 35), dma(2, 35), dma(6), dma(6),
        ],
        compiler_params=pltpu.CompilerParams(
            collective_id=0, has_side_effects=True, vmem_limit_bytes=60 * 1024 * 1024
        ),
    )(forcing, pressure, viscosity, forward, owner)


def solution(mesh):
    placed = (
        P(None, "rad", "lat", "lon"),
        P("rad", "lat", "lon"),
        P("rad", "lat", "lon"),
        P(None, "rad", "lat", "lon"),
        P("rad", "lat", "lon"),
    )
    return jax.shard_map(
        per_device,
        mesh=mesh,
        in_specs=placed,
        out_specs=(P(None, "rad", "lat", "lon"), P("rad", "lat", "lon"), P("rad", "lat", "lon")),
        check_vma=False,
    )
```

time: 126 us -> 93.2 us (0.74)
  Pallas kernels: 118 us -> 89 us
  local copies, waits for them, and re-layouts: 6.55 us -> 3.41 us
    pallas_call x1, Pallas kernels: 118 us -> 89 us  [per_device(): pl.pallas_call(kernel, out_shape=(jax.ShapeDtypeStruct((3, 8, 32, 128), F...]
    unnamed x11 -> x7, local copies, waits for them, and re-layouts: 5.86 us -> 3.41 us
where the time goes in v2:
time: 93.2 us; the launch traced here: 93 us
  Pallas kernels  89 us (95%)
  local copies, waits for them, and re-layouts  3.41 us (4%)
    pallas_call x1, Pallas kernels, per_device(): pl.pallas_call(kernel, out_shape=(jax.ShapeDtypeStruct((3, 8, 32, 128), F...  89 us
    unnamed x7, local copies, waits for them, and re-layouts  3.41 us

profile of v2, /device:TPU:1, one launch (start us, length us, event | category | flops | bytes accessed | tf_op | source)
XLA Modules:
  0.0 93.0 jit_solution(8525048163143646051)
XLA Ops:
  0.6 89.0 %shard_map.76 = (f32[3,8,32,128]{3,2,1,0:T(8,128)}, f32[8,32,128]{2,1,0:T(8,128)}, f32[8,32,128]{2,1,0:T(8,128)}) custom-call(f32[3,8,32,128]{3,2,1,0:T(8,128)} %forcing.1, f32[8,32,128]{2,1,0:T(8,128)} %pressure.1, f32[8,32,128]{2,1,0:T(8,128)} %viscosity.1, f32[3,8,32,128]{3,2,1,0:T(8,128)} %forward.1, s32[2,8,32]{2,1,0:T(8,128)} %owner.1), custom_call_target="tpu_custom_call" | custom-call | tf_op jit(solution)/shard_map/pallas_call | solution.py:952
  89.6 0.0 copy-start.1
  89.6 1.8 %copy.11 = f32[3,8,32,128]{3,2,1,0:T(8,128)} copy(f32[3,8,32,128]{3,2,1,0:T(8,128)} %get-tuple-element.6) | data formatting | bytes 786432
  91.4 0.0 copy-done.1
  91.4 0.0 copy-start
  91.4 0.7 copy.12
  92.1 0.3 copy-done
  92.4 0.7 copy.13
Async XLA Ops:
  89.6 1.8 %copy-start.1 = (f32[8,32,128]{2,1,0:T(8,128)S(1)}, f32[8,32,128]{2,1,0:T(8,128)}, u32[]{:S(2)}) copy-start(f32[8,32,128]{2,1,0:T(8,128)} %get-tuple-element.7) | copy-start | bytes 393220
  91.4 1.0 %copy-start = (f32[8,32,128]{2,1,0:T(8,128)S(1)}, f32[8,32,128]{2,1,0:T(8,128)}, u32[]{:S(2)}) copy-start(f32[8,32,128]{2,1,0:T(8,128)} %get-tuple-element.8) | copy-start | bytes 393220

commit v3 on v2

--- a/solution.py
+++ b/solution.py
@@ -50,12 +50,12 @@
     forcing, pressure, viscosity, forward, owner,
     adjoint, pnext, gradient,
     load, base, fwd, base_z, fwd_z,
-    buf0, zbuf, faces0, faces1, faces2, links0, diag0, inv0, res0, sol0, rim0, hbuf, hz, applied,
+    buf0, zbuf, faces0, faces1, faces2, links0, diag0, inv0, res0, sol0, rim0, hbuf, hz, applied, mbuf, mz,
     coef1, coef2, inv1, inv2, right1, left1, right2, deep1, deep2, sol1, sol2,
-    zsend1, zgot1, dense2, dgot2,
-    tmp, flat, erows, tile, got1, got2, got3,
-    in_sem, send_sem, recv_sem, fsend, frecv, send1, recv1, send2, recv2, send3, recv3,
-    dsend1, drecv1, dsend2, drecv2, hsend, hrecv,
+    zsend1, zgot1, cz, dgot2,
+    tmp, flat, erows, tile, got1, got2, summed, layers, rings,
+    in_sem, send_sem, recv_sem, fsend, frecv, send1, recv1, send2, recv2, sum_send1, sum_recv1, sum_send2, sum_recv2,
+    dsend1, drecv1, dsend2, drecv2, hsend, hrecv, msend, mrecv, csend1, crecv1, csend2, crecv2,
 ):
     me = tuple(lax.axis_index(a) for a in AXES)
     rad, lat, lon = me
@@ -70,13 +70,14 @@
     along = [device(0, 0, k) for k in range(1, 8)]
     across = [device(0, k, 0) for k in range(1, 8)]
     through = [device(k, 0, 0) for k in range(1, 4)]
+    layer = [device(a, b, 0) for a in range(4) for b in range(8) if a or b]
     near1 = [
         (a, b, c) for a in (0, 1, -1) for b in (0, 1, -1) for c in (0, 1, -1) if a or b or c
     ]
     near2 = [
         (a, b, c) for a in range(4) for b in (0, 1, -1) for c in (0, 1, -1) if a or b or c
     ]
-    peers = [device(*o) for o in near2] + along[1:6] + across[1:6]
+    peers = up + down
 
     own_rows = pl.ds(TOP, 32)
     loads = [
@@ -97,6 +98,7 @@
         clear(base, every, plane, slice(8, 40))
         clear(fwd, every, plane, slice(8, 40))
         clear(hbuf, every, plane, slice(8, 40))
+        clear(mbuf, every, plane, slice(8, 40))
     clear(coef1, every, slice(0, 12), low_rows)
     clear(coef1, every, slice(0, 12), slice(32, 48))
     for planes in (slice(0, 4), slice(8, 12)):
@@ -424,16 +426,118 @@
 
         return finish
 
+    def spread_coef1():
+        def go(copies):
+            for start, _ in copies:
+                start()
+
+        def done(copies):
+            for _, wait in copies:
+                wait()
+
+        def copy(i, src, dst, target):
+            return remote(src, dst, csend1.at[i], crecv1.at[i], target)
+
+        ref, planes = coef1, pl.ds(0, 12)
+        in_x = [
+            guarded(copy(0, ref.at[:, pl.ds(5, 3), OWN1], ref.at[:, pl.ds(1, 3), OWN1], up[0]), 1),
+            guarded(copy(1, ref.at[:, pl.ds(4, 4), OWN1], ref.at[:, pl.ds(8, 4), OWN1], down[0]), -1),
+        ]
+        in_y = [
+            plain(copy(2, ref.at[:, planes, pl.ds(28, 4)], ref.at[:, planes, pl.ds(12, 4)], up[1])),
+            plain(copy(3, ref.at[:, planes, pl.ds(16, 4)], ref.at[:, planes, pl.ds(32, 4)], down[1])),
+        ]
+        in_z = [
+            plain(copy(4, cz.at[1], cz.at[2], up[2])),
+            plain(copy(5, cz.at[0], cz.at[3], down[2])),
+        ]
+        parts = [(s, a, g) for s in range(2) for a in range(4) for g in range(4)]
+
+        def pack_pair(t, carry):
+            zlow = zhigh = zero8
+            for j, (s, a, g) in enumerate(parts):
+                part = ref[a, 2 * t + s, pl.ds(8 + 8 * g, 8), :]
+                turned = pltpu.roll(part, 4 * j, 1) if j else part
+                zlow = jnp.where((lane8 >= 4 * j) & (lane8 < 4 * j + 4), turned, zlow)
+                top = (60 + 4 * j) % 128
+                zhigh = jnp.where((lane8 >= top) & (lane8 < top + 4), turned, zhigh)
+            cz[0, t] = zlow
+            cz[1, t] = zhigh
+            return carry
+
+        def unpack_pair(t, carry):
+            below, above = cz[2, t], cz[3, t]
+            for m in range(4):
+                turn_by = (192 - 32 * m) % 128
+                high = pltpu.roll(above, turn_by, 1) if turn_by else above
+                low = pltpu.roll(below, turn_by, 1) if turn_by else below
+                both = jnp.where((lane8 >= 64) & (lane8 < 96), high, low)
+                for j in range(8):
+                    s, a, g = parts[8 * m + j]
+                    side = pltpu.roll(both, 128 - 4 * j, 1) if j else both
+                    rows = pl.ds(8 + 8 * g, 8)
+                    own = ref[a, 2 * t + s, rows, :]
+                    side = jnp.where(side_lanes, side, 0.0)
+                    ref[a, 2 * t + s, rows, :] = jnp.where(lane8 < 64, own, side)
+            return carry
+
+        def first():
+            go(in_x)
+
+        def second():
+            done(in_x)
+            go(in_y)
+
+        def third():
+            done(in_y)
+            lax.fori_loop(0, 6, pack_pair, 0)
+            go(in_z)
+
+        def last():
+            done(in_z)
+            lax.fori_loop(0, 6, unpack_pair, 0)
+
+        return first, second, third, last
+
+    def spread_coef2(tiles):
+        ref = dgot2.at[0]
+        for i, t in enumerate(tiles):
+            ref[rad, 1, 1, i] = t
+
+        def copy(i, src, dst, target):
+            return remote(src, dst, csend2.at[i], crecv2.at[i], target)
+
+        steps = [
+            [copy(i, ref.at[rad, 1, 1], ref.at[rad, 1, 1], target) for i, target in enumerate(through)],
+            [
+                copy(3, ref.at[:, 1, 1], ref.at[:, 0, 1], up[1]),
+                copy(4, ref.at[:, 1, 1], ref.at[:, 2, 1], down[1]),
+            ],
+            [
+                copy(5, ref.at[:, :, 1], ref.at[:, :, 0], up[2]),
+                copy(6, ref.at[:, :, 1], ref.at[:, :, 2], down[2]),
+            ],
+        ]
+
+        def go(i):
+            if i:
+                for c in steps[i - 1]:
+                    c.wait()
+            if i < 3:
+                for c in steps[i]:
+                    c.start()
+
+        return go
+
     def exchange2(use, tiles):
         n = len(tiles)
         for i, t in enumerate(tiles):
-            dense2[use, i] = t
             dgot2[use, rad, 1, 1, i] = t
         copies = []
         for i, (a, b, c) in enumerate(near2):
-            src = dense2.at[use, pl.ds(0, n)]
+            src = dgot2.at[use, rad, 1, 1, pl.ds(0, n)]
             dst = dgot2.at[use, rad, 1 - b, 1 - c, pl.ds(0, n)]
-            copies.append(remote(src, dst, dsend2.at[use, i], drecv2.at[use, i], device(a, b, c)))
+            copies.append(remote(src, dst, dsend2.at[i], drecv2.at[i], device(a, b, c)))
         for copy in copies:
             copy.start()
 
@@ -667,8 +771,9 @@
                 part = jnp.where(row8 == c, row, part)
             value = value + (pltpu.roll(part, 32 * block_x, 1) if block_x else part)
         begin(value)
-        meanwhile()
+        meanwhile[0]()
         middle()
+        meanwhile[1]()
         end()
 
         def all_of(i):
@@ -729,15 +834,19 @@
         for x in range(4):
             for k, value in enumerate(coefficients(1, faces1, x)):
                 coef1[k, 4 + x, OWN1, :] = value
-        pending["coef1"] = exchange1(0, coef1, 3, 4)
+        pending["coef1"] = spread_coef1()
+        pending["coef1"][0]()
 
     def while_second():
+        pending["coef1"][1]()
         coarsen(1, faces1, faces2)
         values = [coefficients(2, faces2, x) for x in range(2)]
         last = jnp.where(rows_of((8, 128)) == 0, runs.astype(F32), pltpu.roll(run_sides(), 1, 0))
         parts = packed2([values[x][k] for k in range(4) for x in range(2)])
-        pending["coef2"] = exchange2(0, parts + [last])
-
+        pending["coef2"] = spread_coef2(parts + [last])
+        pending["coef2"](0)
+
+    def weigh_all():
         def weigh(x, accs):
             v, inv = base[0, x + 1, own_rows, :], inv0[block(x, 32), :]
             parts = [2.0 * inv * (v - faces0[2 * c + 1, block(x, 32), :]) for c in range(3)]
@@ -748,27 +857,52 @@
         accs = lax.fori_loop(0, 8, weigh, (zero8, zero8), unroll=2)
         pending["h"] = send_all(accs, hbuf, hz, hsend, hrecv)
 
+    def applied_to(buf, halo, x):
+        at = block(x, 32)
+        rims = rims_of(halo, 12, x)
+        out = []
+        for c in range(3):
+            v = buf[c, x + 1, own_rows, :]
+            low_z, high_z = shifted(v, rims[4 * c : 4 * c + 4])
+            total = diag0[at, :] * v - links0[0, at, :] * buf[c, x, own_rows, :]
+            total = total - links0[1, at, :] * buf[c, x + 2, own_rows, :]
+            total = total - links0[2, at, :] * buf[c, x + 1, pl.ds(TOP - 1, 32), :]
+            total = total - links0[3, at, :] * buf[c, x + 1, pl.ds(TOP + 1, 32), :]
+            out.append(total - links0[4, at, :] * low_z - links0[5, at, :] * high_z)
+        return out
+
     def apply_to_h():
         halo = pending["h"]()
 
+        def one(x, accs):
+            at = block(x, 32)
+            v, inv = base[0, x + 1, own_rows, :], inv0[at, :]
+            parts = []
+            for c, g in enumerate(applied_to(hbuf, halo, x)):
+                u = (1.0 + STEPS[1][0]) * 2.0 * (v - faces0[2 * c + 1, at, :]) - STEPS[1][1] * g
+                applied[c, at, :] = u
+                m = STEPS[0][1] * inv * u + STEPS[1][1] * hbuf[c, x + 1, own_rows, :]
+                mbuf[c, x + 1, own_rows, :] = m
+                parts.append(m)
+            return pack(accs, parts, x)
+
+        accs = lax.fori_loop(0, 8, one, (zero8, zero8))
+        pending["m"] = send_all(accs, mbuf, mz, msend, mrecv)
+
+    def apply_to_m():
+        halo = pending["m"]()
+
         def one(x, carry):
             at = block(x, 32)
-            rims = rims_of(halo, 12, x)
-            for c in range(3):
-                v = hbuf[c, x + 1, own_rows, :]
-                low_z, high_z = shifted(v, rims[4 * c : 4 * c + 4])
-                total = diag0[at, :] * v - links0[0, at, :] * hbuf[c, x, own_rows, :]
-                total = total - links0[1, at, :] * hbuf[c, x + 2, own_rows, :]
-                total = total - links0[2, at, :] * hbuf[c, x + 1, pl.ds(TOP - 1, 32), :]
-                total = total - links0[3, at, :] * hbuf[c, x + 1, pl.ds(TOP + 1, 32), :]
-                applied[c, at, :] = total - links0[4, at, :] * low_z - links0[5, at, :] * high_z
+            for c, g in enumerate(applied_to(mbuf, halo, x)):
+                applied[c, at, :] = STEPS[0][0] * applied[c, at, :] - g
             return carry
 
-        lax.fori_loop(0, 8, one, 0, unroll=2)
+        lax.fori_loop(0, 8, one, 0)
 
     def while_third():
-        pending["coef1"](0, 12)
-        invert(coef1, inv1, 12)
+        pending["coef1"][2]()
+        pending["coef2"](1)
 
     accs = start
     for step, meanwhile in ((STEPS[0], while_first), (STEPS[1], while_second), (None, while_third)):
@@ -781,10 +915,11 @@
     for c in range(3):
         for x in range(4):
             right1[c, 4 + x, OWN1, :] = sums[64 * c + 16 * x : 64 * c + 16 * x + 16]
-    finish = exchange1(1, right1, 3, 3)
-    pending["coef2"]()
-    unpack2(0, coef2)
-    invert(coef2, inv2, 12)
+    finish = exchange1(0, right1, 3, 3)
+    pending["coef1"][3]()
+    invert(coef1, inv1, 12)
+    pending["coef2"](2)
+    weigh_all()
     finish(1, 11)
     begin_deep(1, right1, (1, 11), None)
     sweep_deep(1, 0, right1, right1, (2, 10), STEPS[0])
@@ -793,7 +928,10 @@
 
     sums = restrict(lambda c, x: left1[c, 4 + x, OWN1, :], 16, 1, own_pair)
     finish2 = exchange2(1, packed2([sums[16 * c + 8 * x : 16 * c + 8 * x + 8] for c in range(3) for x in range(2)]))
-    finish1 = exchange1(2, left1, 3, 3)
+    finish1 = exchange1(1, left1, 3, 3)
+    pending["coef2"](3)
+    unpack2(0, coef2)
+    invert(coef2, inv2, 12)
     apply_to_h()
     finish2()
     unpack2(1, right2)
@@ -802,7 +940,7 @@
     sweep_deep(2, 0, right2, right2, all2, STEPS[0])
     sweep_deep(2, 1, right2, right2, all2, STEPS[1])
     sweep_deep(2, 0, right2, right2, all2, None)
-    coarse_solve(lambda: finish1(1, 11))
+    coarse_solve((lambda: finish1(1, 11), apply_to_m))
     sweep_deep(2, 1, right2, right2, all2, STEPS[0], initial=True)
     sweep_deep(2, 0, right2, right2, all2, STEPS[0])
     sweep_deep(2, 1, right2, right2, all2, STEPS[1])
@@ -853,24 +991,44 @@
 
     accs = sweep(p, None, STEPS[0], initial=True)
     p = turn[0] % 2
-    accs = sweep(p, exchange(accs)(), STEPS[0])
-    p = turn[0] % 2
     finish = exchange(accs)
-    begin, middle, end = gather(1)
 
     def add_up(x, total):
         at = block(x, 32)
         v = base[0, x + 1, own_rows, :]
         part = base[1, x + 1, own_rows, :]
         for c in range(3):
-            update = buf0[p, c, x + 1, own_rows, :]
-            weight = 2.0 * (v - faces0[2 * c + 1, at, :])
-            h = hbuf[c, x + 1, own_rows, :]
-            part = part - weight * (sol0[c, at, :] + STEPS[1][0] * update)
-            part = part - STEPS[1][1] * (h * res0[c, at, :] - applied[c, at, :] * update)
+            part = part - 2.0 * (v - faces0[2 * c + 1, at, :]) * sol0[c, at, :]
+            part = part - mbuf[c, x + 1, own_rows, :] * res0[c, at, :]
+            part = part - applied[c, at, :] * buf0[p, c, x + 1, own_rows, :]
         return total + (part[0:8] + part[8:16] + part[16:24] + part[24:32])
 
-    begin(lax.fori_loop(0, 8, add_up, zero8, unroll=2))
+    partial = lax.fori_loop(0, 8, add_up, zero8, unroll=2)
+    sums1 = [
+        remote(summed.at[0], layers.at[rad, lat], sum_send1.at[i], sum_recv1.at[i], target)
+        for i, target in enumerate(layer)
+    ]
+    sums2 = [
+        remote(summed.at[1], rings.at[lon], sum_send2.at[i], sum_recv2.at[i], target)
+        for i, target in enumerate(along)
+    ]
+    summed[0] = partial
+    layers[rad, lat] = partial
+    for copy in sums1:
+        copy.start()
+    accs = sweep(p, finish(), STEPS[0])
+    p = turn[0] % 2
+    finish = exchange(accs)
+    for copy in sums1:
+        copy.wait()
+    total = zero8
+    for a in range(4):
+        for b in range(8):
+            total = total + layers[a, b]
+    summed[1] = total
+    rings[lon] = total
+    for copy in sums2:
+        copy.start()
     final = 1 - p
 
     def emit(afters, x):
@@ -883,7 +1041,6 @@
     finish = exchange(accs)
     for _, wait in fwd_copies:
         wait()
-    middle()
     halo = finish()
     fwd_halo = merged(zero8, fwd_z[1])
 
@@ -921,22 +1078,13 @@
         gradient[x] = 2.0 * v * summed
         return carry
 
-    end()
-    total = zero8
-    for b in range(8):
-        total = total + got2[1, 8 * b : 8 * b + 8, :]
-    tile[1, 2] = total
-    got3[rad] = total
-    last = [
-        remote(tile.at[1, 2], got3.at[rad], send3.at[i], recv3.at[i], target)
-        for i, target in enumerate(through)
-    ]
-    for copy in last:
-        copy.start()
     lax.fori_loop(0, 8, outputs, 0, unroll=2)
-    for copy in last:
+    for copy in sums2:
         copy.wait()
-    mean = jnp.sum(got3[0] + got3[1] + got3[2] + got3[3]) / CELLS
+    total = rings[0]
+    for k in range(1, 8):
+        total = total + rings[k]
+    mean = jnp.sum(total) / CELLS
 
     def shift(x, carry):
         pnext[x] = pnext[x] - mean
@@ -962,15 +1110,15 @@
             f32(3, 8, 32, 128), f32(2, 10, 48, 128), f32(3, 10, 48, 128), f32(1, 8, 128), f32(2, 8, 128),
             f32(2, 3, 10, 48, 128), f32(2, 4, 8, 128), f32(6, 256, 128), f32(6, 64, 128), f32(6, 16, 128),
             f32(6, 256, 128), f32(256, 128), f32(256, 128), f32(3, 256, 128), f32(3, 256, 128), f32(3, 8, 32, 128),
-            f32(3, 10, 48, 128), f32(4, 8, 128), f32(3, 256, 128),
+            f32(3, 10, 48, 128), f32(4, 8, 128), f32(3, 256, 128), f32(3, 10, 48, 128), f32(4, 8, 128),
             f32(4, 13, 48, 128), f32(4, 12, 40, 128), f32(12, 48, 128), f32(12, 40, 128),
             f32(3, 12, 48, 128), f32(3, 12, 48, 128), f32(3, 12, 40, 128),
             f32(2, 3, 12, 48, 128), f32(2, 3, 12, 40, 128), f32(3, 12, 48, 128), f32(3, 12, 40, 128),
-            f32(3, 2, 8, 128), f32(3, 3, 3, 2, 8, 128), f32(2, 3, 8, 128), f32(2, 4, 3, 3, 3, 8, 128),
-            f32(6, 48, 128), f32(6, 144, 128), f32(3, 8, 128), f32(2, 3, 8, 128),
-            f32(2, 8, 8, 128), f32(2, 64, 128), f32(4, 8, 128),
-            dma(4), dma(2, 6), dma(2, 6), dma(3), dma(3), dma(2, 7), dma(2, 7), dma(2, 7), dma(2, 7), dma(3), dma(3),
-            dma(3, 26), dma(3, 26), dma(2, 35), dma(2, 35), dma(6), dma(6),
+            f32(2, 2, 8, 128), f32(2, 3, 3, 2, 8, 128), f32(4, 6, 8, 128), f32(2, 4, 3, 3, 3, 8, 128),
+            f32(6, 48, 128), f32(6, 144, 128), f32(3, 8, 128), f32(1, 2, 8, 128),
+            f32(1, 8, 8, 128), f32(1, 64, 128), f32(2, 8, 128), f32(4, 8, 8, 128), f32(8, 8, 128),
+            dma(4), dma(2, 6), dma(2, 6), dma(3), dma(3), dma(1, 7), dma(1, 7), dma(1, 7), dma(1, 7), dma(31), dma(31), dma(7), dma(7),
+            dma(2, 26), dma(2, 26), dma(35), dma(35), dma(6), dma(6), dma(6), dma(6), dma(6), dma(6), dma(7), dma(7),
         ],
         compiler_params=pltpu.CompilerParams(
             collective_id=0, has_side_effects=True, vmem_limit_bytes=60 * 1024 * 1024

time: 93.2 us -> 84.2 us (0.903)
  Pallas kernels: 89 us -> 80 us
    pallas_call x1, Pallas kernels: 89 us -> 80 us  [per_device(): pl.pallas_call(kernel, out_shape=(jax.ShapeDtypeStruct((3, 8, 32, 128), F...]
where the time goes in v3:
time: 84.2 us; the launch traced here: 84.1 us
  Pallas kernels  80 us (95%)
  local copies, waits for them, and re-layouts  3.41 us (4%)
    pallas_call x1, Pallas kernels, per_device(): pl.pallas_call(kernel, out_shape=(jax.ShapeDtypeStruct((3, 8, 32, 128), F...  80 us
    unnamed x7, local copies, waits for them, and re-layouts  3.41 us

profile of v3, /device:TPU:1, one launch (start us, length us, event | category | flops | bytes accessed | tf_op | source)
XLA Modules:
  0.0 84.1 jit_solution(12221120472751662768)
XLA Ops:
  0.6 80.0 %shard_map.76 = (f32[3,8,32,128]{3,2,1,0:T(8,128)}, f32[8,32,128]{2,1,0:T(8,128)}, f32[8,32,128]{2,1,0:T(8,128)}) custom-call(f32[3,8,32,128]{3,2,1,0:T(8,128)} %forcing.1, f32[8,32,128]{2,1,0:T(8,128)} %pressure.1, f32[8,32,128]{2,1,0:T(8,128)} %viscosity.1, f32[3,8,32,128]{3,2,1,0:T(8,128)} %forward.1, s32[2,8,32]{2,1,0:T(8,128)} %owner.1), custom_call_target="tpu_custom_call" | custom-call | tf_op jit(solution)/shard_map/pallas_call | solution.py:1100
  80.6 0.0 copy-start.1
  80.6 1.8 %copy.11 = f32[3,8,32,128]{3,2,1,0:T(8,128)} copy(f32[3,8,32,128]{3,2,1,0:T(8,128)} %get-tuple-element.6) | data formatting | bytes 786432
  82.5 0.0 copy-done.1
  82.5 0.0 copy-start
  82.5 0.7 copy.12
  83.1 0.3 copy-done
  83.4 0.7 copy.13
Async XLA Ops:
  80.6 1.8 %copy-start.1 = (f32[8,32,128]{2,1,0:T(8,128)S(1)}, f32[8,32,128]{2,1,0:T(8,128)}, u32[]{:S(2)}) copy-start(f32[8,32,128]{2,1,0:T(8,128)} %get-tuple-element.7) | copy-start | bytes 393220
  82.5 1.0 %copy-start = (f32[8,32,128]{2,1,0:T(8,128)S(1)}, f32[8,32,128]{2,1,0:T(8,128)}, u32[]{:S(2)}) copy-start(f32[8,32,128]{2,1,0:T(8,128)} %get-tuple-element.8) | copy-start | bytes 393220

commit v4 on v3

--- a/solution.py
+++ b/solution.py
@@ -51,10 +51,11 @@
     adjoint, pnext, gradient,
     load, base, fwd, base_z, fwd_z,
     buf0, zbuf, faces0, faces1, faces2, links0, diag0, inv0, res0, sol0, rim0, hbuf, hz, applied, mbuf, mz,
+    wide0, rim_link, halo_x, halo_y,
     coef1, coef2, inv1, inv2, right1, left1, right2, deep1, deep2, sol1, sol2,
     zsend1, zgot1, cz, dgot2,
-    tmp, flat, erows, tile, got1, got2, summed, layers, rings,
-    in_sem, send_sem, recv_sem, fsend, frecv, send1, recv1, send2, recv2, sum_send1, sum_recv1, sum_send2, sum_recv2,
+    tmp, flat, erows, tile, got1, got2, summed, sum_x, sum_y, sum_z,
+    in_sem, send_sem, recv_sem, fsend, frecv, send1, recv1, send2, recv2, sum_send, sum_recv,
     dsend1, drecv1, dsend2, drecv2, hsend, hrecv, msend, mrecv, csend1, crecv1, csend2, crecv2,
 ):
     me = tuple(lax.axis_index(a) for a in AXES)
@@ -67,15 +68,14 @@
 
     up = [device(1, 0, 0), device(0, 1, 0), device(0, 0, 1)]
     down = [device(-1, 0, 0), device(0, -1, 0), device(0, 0, -1)]
-    along = [device(0, 0, k) for k in range(1, 8)]
-    across = [device(0, k, 0) for k in range(1, 8)]
+    along = [device(0, 0, k) for k in (4, 3, 5, 2, 6, 1, 7)]
+    across = [device(0, k, 0) for k in (4, 3, 5, 2, 6, 1, 7)]
     through = [device(k, 0, 0) for k in range(1, 4)]
-    layer = [device(a, b, 0) for a in range(4) for b in range(8) if a or b]
     near1 = [
-        (a, b, c) for a in (0, 1, -1) for b in (0, 1, -1) for c in (0, 1, -1) if a or b or c
+        (a, b, c) for c in (1, -1, 0) for b in (1, -1, 0) for a in (1, -1, 0) if a or b or c
     ]
     near2 = [
-        (a, b, c) for a in range(4) for b in (0, 1, -1) for c in (0, 1, -1) if a or b or c
+        (a, b, c) for c in (1, -1, 0) for a in (2, 1, 3, 0) for b in (1, -1, 0) if a or b or c
     ]
     peers = up + down
 
@@ -94,11 +94,21 @@
 
     every, low_rows, high_rows = slice(None), slice(8, 16), slice(32, 40)
     for plane in (0, 9):
-        clear(buf0, every, every, plane, slice(8, 40))
         clear(base, every, plane, slice(8, 40))
         clear(fwd, every, plane, slice(8, 40))
+
+    barrier = pltpu.get_barrier_semaphore()
+    for target in peers:
+        pl.semaphore_signal(barrier, inc=1, device_id=target, device_id_type=MESH)
+
+    for plane in (0, 9):
+        clear(buf0, every, every, plane, slice(8, 40))
+        clear(halo_x, every, plane // 9)
+        clear(halo_y, every, plane // 9)
         clear(hbuf, every, plane, slice(8, 40))
         clear(mbuf, every, plane, slice(8, 40))
+    clear(buf0, every, every, slice(1, 9), slice(0, 8))
+    clear(buf0, every, every, slice(1, 9), slice(40, 48))
     clear(coef1, every, slice(0, 12), low_rows)
     clear(coef1, every, slice(0, 12), slice(32, 48))
     for planes in (slice(0, 4), slice(8, 12)):
@@ -121,10 +131,6 @@
     for side in (0, 2):
         clear(zgot1, every, side)
 
-    barrier = pltpu.get_barrier_semaphore()
-    for target in peers:
-        pl.semaphore_signal(barrier, inc=1, device_id=target, device_id_type=MESH)
-
     def remote(src, dst, ssem, rsem, target):
         return pltpu.make_async_remote_copy(
             src_ref=src, dst_ref=dst, send_sem=ssem, recv_sem=rsem,
@@ -183,13 +189,18 @@
     def plain(copy):
         return copy.start, copy.wait
 
-    def sends(buf, zref, ssem, rsem):
+    def sends(buf, zref, ssem, rsem, beside=None):
         rows, planes = pl.ds(TOP, 32), pl.ds(1, 8)
+        if beside is None:
+            to = [buf.at[:, 0, rows], buf.at[:, 9, rows], buf.at[:, planes, pl.ds(TOP - 1, 1)], buf.at[:, planes, pl.ds(TOP + 32, 1)]]
+        else:
+            in_x, in_y = beside
+            to = [in_x.at[0], in_x.at[1], in_y.at[0, :, :, pl.ds(0, 1)], in_y.at[1, :, :, pl.ds(7, 1)]]
         parts = [
-            (buf.at[:, 8, rows], buf.at[:, 0, rows], up[0]),
-            (buf.at[:, 1, rows], buf.at[:, 9, rows], down[0]),
-            (buf.at[:, planes, pl.ds(TOP + 31, 1)], buf.at[:, planes, pl.ds(TOP - 1, 1)], up[1]),
-            (buf.at[:, planes, pl.ds(TOP, 1)], buf.at[:, planes, pl.ds(TOP + 32, 1)], down[1]),
+            (buf.at[:, 8, rows], to[0], up[0]),
+            (buf.at[:, 1, rows], to[1], down[0]),
+            (buf.at[:, planes, pl.ds(TOP + 31, 1)], to[2], up[1]),
+            (buf.at[:, planes, pl.ds(TOP, 1)], to[3], down[1]),
             (zref.at[1], zref.at[2], up[2]),
             (zref.at[0], zref.at[3], down[2]),
         ]
@@ -197,13 +208,13 @@
             remote(src, dst, ssem.at[i], rsem.at[i], target)
             for i, (src, dst, target) in enumerate(parts)
         ]
-        return [guarded(copies[0], 1), guarded(copies[1], -1)] + [plain(copy) for copy in copies[2:]]
+        return [plain(copy) for copy in copies[4:]] + [guarded(copies[0], 1), guarded(copies[1], -1)] + [plain(copy) for copy in copies[2:4]]
 
     turn = [0]
 
-    def send_all(accs, buf, zref, ssem, rsem):
+    def send_all(accs, buf, zref, ssem, rsem, beside=None):
         zref[0], zref[1] = accs
-        copies = sends(buf, zref, ssem, rsem)
+        copies = sends(buf, zref, ssem, rsem, beside)
         for start, _ in copies:
             start()
 
@@ -217,7 +228,8 @@
     def exchange(accs, buf=None):
         p = turn[0] % 2
         turn[0] += 1
-        return send_all(accs, buf0.at[p] if buf is None else buf, zbuf.at[p], send_sem.at[p], recv_sem.at[p])
+        sems = (zbuf.at[p], send_sem.at[p], recv_sem.at[p])
+        return send_all(accs, buf0.at[p], *sems, (halo_x.at[p], halo_y.at[p])) if buf is None else send_all(accs, buf, *sems)
 
     for copy in loads[:2]:
         copy.wait()
@@ -287,7 +299,8 @@
             faces0[k, at, :] = six[k]
         masks = (lower_x, upper_x, lower_y, upper_y)
         for k in range(6):
-            links0[k, at, :] = six[k] * masks[k] if k < 4 else six[k]
+            links0[k, at, :] = six[k] * masks[k] if k < 4 else jnp.where(lane32 == (0, 127)[k - 4], 0.0, six[k])
+        rim_link[at, :] = jnp.where(lane32 == 0, six[4], jnp.where(lane32 == 127, six[5], 0.0))
         diag = six[0] + six[1] + six[2] + six[3] + six[4] + six[5]
         inv = 1.0 / diag
         diag0[at, :] = diag
@@ -304,7 +317,6 @@
             right = load[c, x] - grads[c]
             res0[c, at, :] = right
             update = inv * right * FIRST
-            sol0[c, at, :] = update
             buf0[1, c, x + 1, own_rows, :] = update
             updates.append(update)
         return pack(accs, updates, x)
@@ -422,11 +434,13 @@
                             ref[a, plane, rows, :] = jnp.where(lane8 < 64, own, side)
                 return carry
 
-            lax.fori_loop(low_plane, high_plane, one, 0)
+            lax.fori_loop(low_plane, high_plane, one, 0, unroll=2)
 
         return finish
 
-    def spread_coef1():
+    def layers1(use, ref, depth_up, depth_down):
+        n = ref.shape[0]
+
         def go(copies):
             for start, _ in copies:
                 start()
@@ -436,22 +450,23 @@
                 wait()
 
         def copy(i, src, dst, target):
-            return remote(src, dst, csend1.at[i], crecv1.at[i], target)
-
-        ref, planes = coef1, pl.ds(0, 12)
+            return remote(src, dst, csend1.at[use, i], crecv1.at[use, i], target)
+
+        planes, zs = pl.ds(0, 12), cz.at[use]
+        up_x, down_x = (pl.ds(8 - depth_up, depth_up), pl.ds(4 - depth_up, depth_up)), (pl.ds(4, depth_down), pl.ds(8, depth_down))
         in_x = [
-            guarded(copy(0, ref.at[:, pl.ds(5, 3), OWN1], ref.at[:, pl.ds(1, 3), OWN1], up[0]), 1),
-            guarded(copy(1, ref.at[:, pl.ds(4, 4), OWN1], ref.at[:, pl.ds(8, 4), OWN1], down[0]), -1),
+            guarded(copy(0, ref.at[:, up_x[0], OWN1], ref.at[:, up_x[1], OWN1], up[0]), 1),
+            guarded(copy(1, ref.at[:, down_x[0], OWN1], ref.at[:, down_x[1], OWN1], down[0]), -1),
         ]
         in_y = [
             plain(copy(2, ref.at[:, planes, pl.ds(28, 4)], ref.at[:, planes, pl.ds(12, 4)], up[1])),
             plain(copy(3, ref.at[:, planes, pl.ds(16, 4)], ref.at[:, planes, pl.ds(32, 4)], down[1])),
         ]
         in_z = [
-            plain(copy(4, cz.at[1], cz.at[2], up[2])),
-            plain(copy(5, cz.at[0], cz.at[3], down[2])),
+            plain(copy(4, zs.at[1], zs.at[2], up[2])),
+            plain(copy(5, zs.at[0], zs.at[3], down[2])),
         ]
-        parts = [(s, a, g) for s in range(2) for a in range(4) for g in range(4)]
+        parts = [(s, a, g) for s in range(2) for a in range(n) for g in range(4)]
 
         def pack_pair(t, carry):
             zlow = zhigh = zero8
@@ -461,13 +476,13 @@
                 zlow = jnp.where((lane8 >= 4 * j) & (lane8 < 4 * j + 4), turned, zlow)
                 top = (60 + 4 * j) % 128
                 zhigh = jnp.where((lane8 >= top) & (lane8 < top + 4), turned, zhigh)
-            cz[0, t] = zlow
-            cz[1, t] = zhigh
+            zs[0, t] = zlow
+            zs[1, t] = zhigh
             return carry
 
         def unpack_pair(t, carry):
-            below, above = cz[2, t], cz[3, t]
-            for m in range(4):
+            below, above = zs[2, t], zs[3, t]
+            for m in range(n):
                 turn_by = (192 - 32 * m) % 128
                 high = pltpu.roll(above, turn_by, 1) if turn_by else above
                 low = pltpu.roll(below, turn_by, 1) if turn_by else below
@@ -625,44 +640,79 @@
 
         lax.fori_loop(planes[0], planes[1], one, 0, unroll=2)
 
-    def sweep(p, halo, step, initial=False, emit=None):
+    def inside(p, first=False):
+        def plane(x, carry):
+            at = block(x, 32)
+            diag = diag0[at, :]
+            ls = [links0[k, at, :] for k in range(6)]
+            for c in range(3):
+                v = buf0[p, c, x + 1, own_rows, :]
+                total = diag * v - ls[0] * buf0[p, c, x, own_rows, :]
+                total = total - ls[1] * buf0[p, c, x + 2, own_rows, :]
+                total = total - ls[2] * buf0[p, c, x + 1, pl.ds(TOP - 1, 32), :]
+                total = total - ls[3] * buf0[p, c, x + 1, pl.ds(TOP + 1, 32), :]
+                total = total - ls[4] * pltpu.roll(v, 1, 1) - ls[5] * pltpu.roll(v, 127, 1)
+                res0[c, at, :] = res0[c, at, :] - total
+                sol0[c, at, :] = v if first else sol0[c, at, :] + v
+            return carry
+
+        lax.fori_loop(0, 8, plane, 0, unroll=2)
+
+    def rim_terms(p, halo, step, emit=None):
+        for side, rows in ((0, pl.ds(0, 32)), (1, pl.ds(224, 32))):
+            link = links0[side, rows, :]
+            for c in range(3):
+                res0[c, rows, :] = res0[c, rows, :] + link * halo_x[p, side, c]
+
+        def plane(x, accs):
+            at = block(x, 32)
+            inv, rim = inv0[at, :], rim_link[at, :]
+            low_y, high_y = links0[2, block(4 * x, 8), :], links0[3, block(4 * x + 3, 8), :]
+            rims = rims_of(halo, 12, x)
+            packs = []
+            for c in range(3):
+                r = res0[c, at, :] + rim * jnp.concatenate(rims[4 * c : 4 * c + 4], 0)
+                top = r[0:8] + low_y * halo_y[p, 0, c, x]
+                bottom = r[24:32] + high_y * halo_y[p, 1, c, x]
+                r = jnp.concatenate([top, r[8:24], bottom], 0)
+                if emit is None:
+                    res0[c, at, :] = r
+                if step is None:
+                    continue
+                update = step[0] * buf0[p, c, x + 1, own_rows, :] + step[1] * inv * r
+                if emit is None:
+                    buf0[1 - p, c, x + 1, own_rows, :] = update
+                    packs.append(update)
+                else:
+                    packs.append(sol0[c, at, :] + update)
+            if step is None:
+                return accs
+            if emit is not None:
+                emit(packs, x)
+            return pack(accs, packs, x)
+
+        return lax.fori_loop(0, 8, plane, (zero8, zero8), unroll=2)
+
+    def correct(p):
         def plane(x, accs):
             at = block(x, 32)
             diag, inv = diag0[at, :], inv0[at, :]
             ls = [links0[k, at, :] for k in range(6)]
-            rims = rims_of(halo, 12, x) if halo is not None else None
             packs = []
             for c in range(3):
-                v = buf0[p, c, x + 1, own_rows, :]
-                low_z, high_z = shifted(v, rims[4 * c : 4 * c + 4] if rims else rim0[c, x])
-                total = diag * v - ls[0] * buf0[p, c, x, own_rows, :]
-                total = total - ls[1] * buf0[p, c, x + 2, own_rows, :]
-                total = total - ls[2] * buf0[p, c, x + 1, pl.ds(TOP - 1, 32), :]
-                total = total - ls[3] * buf0[p, c, x + 1, pl.ds(TOP + 1, 32), :]
-                total = total - ls[4] * low_z - ls[5] * high_z
-                r = res0[c, at, :] - total
-                if step is None:
-                    res0[c, at, :] = r
-                    continue
-                if initial:
-                    update = FIRST * inv * r
-                    after = sol0[c, at, :] + v + update
-                else:
-                    update = step[0] * v + step[1] * inv * r
-                    after = sol0[c, at, :] + update
-                if emit is None:
-                    sol0[c, at, :] = after
-                    res0[c, at, :] = r
-                    buf0[1 - p, c, x + 1, own_rows, :] = update
-                    packs.append(update)
-                else:
-                    packs.append(after)
-            if step is None:
-                return accs
-            low, high = pack(accs, packs, x)
-            if emit is not None:
-                emit(packs, x)
-            return low, high
+                v = wide0[c, x + 1, own_rows, :]
+                total = diag * v - ls[0] * wide0[c, x, own_rows, :]
+                total = total - ls[1] * wide0[c, x + 2, own_rows, :]
+                total = total - ls[2] * wide0[c, x + 1, pl.ds(TOP - 1, 32), :]
+                total = total - ls[3] * wide0[c, x + 1, pl.ds(TOP + 1, 32), :]
+                total = total - ls[4] * pltpu.roll(v, 1, 1) - ls[5] * pltpu.roll(v, 127, 1)
+                r = res0[c, at, :] - total + rim_link[at, :] * rim0[c, x]
+                res0[c, at, :] = r
+                sol0[c, at, :] = sol0[c, at, :] + v
+                update = FIRST * inv * r
+                buf0[p, c, x + 1, own_rows, :] = update
+                packs.append(update)
+            return pack(accs, packs, x)
 
         return lax.fori_loop(0, 8, plane, (zero8, zero8), unroll=2)
 
@@ -834,7 +884,7 @@
         for x in range(4):
             for k, value in enumerate(coefficients(1, faces1, x)):
                 coef1[k, 4 + x, OWN1, :] = value
-        pending["coef1"] = spread_coef1()
+        pending["coef1"] = layers1(0, coef1, 3, 4)
         pending["coef1"][0]()
 
     def while_second():
@@ -863,12 +913,12 @@
         out = []
         for c in range(3):
             v = buf[c, x + 1, own_rows, :]
-            low_z, high_z = shifted(v, rims[4 * c : 4 * c + 4])
             total = diag0[at, :] * v - links0[0, at, :] * buf[c, x, own_rows, :]
             total = total - links0[1, at, :] * buf[c, x + 2, own_rows, :]
             total = total - links0[2, at, :] * buf[c, x + 1, pl.ds(TOP - 1, 32), :]
             total = total - links0[3, at, :] * buf[c, x + 1, pl.ds(TOP + 1, 32), :]
-            out.append(total - links0[4, at, :] * low_z - links0[5, at, :] * high_z)
+            total = total - links0[4, at, :] * pltpu.roll(v, 1, 1) - links0[5, at, :] * pltpu.roll(v, 127, 1)
+            out.append(total - rim_link[at, :] * jnp.concatenate(rims[4 * c : 4 * c + 4], 0))
         return out
 
     def apply_to_h():
@@ -886,7 +936,7 @@
                 parts.append(m)
             return pack(accs, parts, x)
 
-        accs = lax.fori_loop(0, 8, one, (zero8, zero8))
+        accs = lax.fori_loop(0, 8, one, (zero8, zero8), unroll=2)
         pending["m"] = send_all(accs, mbuf, mz, msend, mrecv)
 
     def apply_to_m():
@@ -898,7 +948,7 @@
                 applied[c, at, :] = STEPS[0][0] * applied[c, at, :] - g
             return carry
 
-        lax.fori_loop(0, 8, one, 0)
+        lax.fori_loop(0, 8, one, 0, unroll=2)
 
     def while_third():
         pending["coef1"][2]()
@@ -908,8 +958,9 @@
     for step, meanwhile in ((STEPS[0], while_first), (STEPS[1], while_second), (None, while_third)):
         p = turn[0] % 2
         finish = exchange(accs)
+        inside(p, meanwhile is while_first)
         meanwhile()
-        accs = sweep(p, finish(), step)
+        accs = rim_terms(p, finish(), step)
 
     sums = restrict(lambda c, x: res0[c, block(x, 32), :], 32, 0, pair)
     for c in range(3):
@@ -928,11 +979,13 @@
 
     sums = restrict(lambda c, x: left1[c, 4 + x, OWN1, :], 16, 1, own_pair)
     finish2 = exchange2(1, packed2([sums[16 * c + 8 * x : 16 * c + 8 * x + 8] for c in range(3) for x in range(2)]))
-    finish1 = exchange1(1, left1, 3, 3)
+    rest = layers1(1, left1, 3, 3)
+    rest[0]()
     pending["coef2"](3)
     unpack2(0, coef2)
     invert(coef2, inv2, 12)
     apply_to_h()
+    rest[1]()
     finish2()
     unpack2(1, right2)
     all2 = (2, 10)
@@ -940,7 +993,12 @@
     sweep_deep(2, 0, right2, right2, all2, STEPS[0])
     sweep_deep(2, 1, right2, right2, all2, STEPS[1])
     sweep_deep(2, 0, right2, right2, all2, None)
-    coarse_solve((lambda: finish1(1, 11), apply_to_m))
+
+    def while_along():
+        rest[2]()
+        apply_to_m()
+
+    coarse_solve((while_along, rest[3]))
     sweep_deep(2, 1, right2, right2, all2, STEPS[0], initial=True)
     sweep_deep(2, 0, right2, right2, all2, STEPS[0])
     sweep_deep(2, 1, right2, right2, all2, STEPS[1])
@@ -967,8 +1025,6 @@
     sweep_deep(1, 0, left1, left1, (2, 10), STEPS[0])
     sweep_deep(1, 1, left1, left1, (3, 9), STEPS[1])
 
-    p = turn[0] % 2
-    turn[0] += 1
     for c in range(3):
         flat[c] = times(sol1[c, 3:9, 12:36, :].reshape(144, 128), spread0)
 
@@ -985,12 +1041,12 @@
         for c in range(3):
             for at in (2 * k - 1, 2 * k):
                 if 0 <= at <= 9:
-                    buf0[p, c, at] = tmp[c, pl.ds(0, 48), :]
+                    wide0[c, at] = tmp[c, pl.ds(0, 48), :]
                 if 1 <= at <= 8:
                     rim0[c, at - 1] = tmp[3 + c, pl.ds(0, 32), :]
 
-    accs = sweep(p, None, STEPS[0], initial=True)
     p = turn[0] % 2
+    accs = correct(p)
     finish = exchange(accs)
 
     def add_up(x, total):
@@ -998,47 +1054,53 @@
         v = base[0, x + 1, own_rows, :]
         part = base[1, x + 1, own_rows, :]
         for c in range(3):
-            part = part - 2.0 * (v - faces0[2 * c + 1, at, :]) * sol0[c, at, :]
-            part = part - mbuf[c, x + 1, own_rows, :] * res0[c, at, :]
-            part = part - applied[c, at, :] * buf0[p, c, x + 1, own_rows, :]
+            update = buf0[p, c, x + 1, own_rows, :]
+            part = part - 2.0 * (v - faces0[2 * c + 1, at, :]) * (sol0[c, at, :] + update)
+            part = part - mbuf[c, x + 1, own_rows, :] * res0[c, at, :] - applied[c, at, :] * update
         return total + (part[0:8] + part[8:16] + part[16:24] + part[24:32])
 
     partial = lax.fori_loop(0, 8, add_up, zero8, unroll=2)
-    sums1 = [
-        remote(summed.at[0], layers.at[rad, lat], sum_send1.at[i], sum_recv1.at[i], target)
-        for i, target in enumerate(layer)
-    ]
-    sums2 = [
-        remote(summed.at[1], rings.at[lon], sum_send2.at[i], sum_recv2.at[i], target)
-        for i, target in enumerate(along)
-    ]
-    summed[0] = partial
-    layers[rad, lat] = partial
-    for copy in sums1:
-        copy.start()
-    accs = sweep(p, finish(), STEPS[0])
+    rounds = []
+    for i, (got, at, targets) in enumerate(((sum_x, rad, through), (sum_y, lat, across), (sum_z, lon, along))):
+        copies = [
+            remote(summed.at[i], got.at[at], sum_send.at[i, k], sum_recv.at[i, k], target)
+            for k, target in enumerate(targets)
+        ]
+        rounds.append((got, at, copies))
+
+    def send_sum(i, value):
+        got, at, copies = rounds[i]
+        summed[i] = value
+        got[at] = value
+        for copy in copies:
+            copy.start()
+
+    def get_sum(i):
+        got, _, copies = rounds[i]
+        for copy in copies:
+            copy.wait()
+        total = got[0]
+        for k in range(1, len(copies) + 1):
+            total = total + got[k]
+        return total
+
+    send_sum(0, partial)
+    inside(p)
+    accs = rim_terms(p, finish(), STEPS[0])
     p = turn[0] % 2
     finish = exchange(accs)
-    for copy in sums1:
-        copy.wait()
-    total = zero8
-    for a in range(4):
-        for b in range(8):
-            total = total + layers[a, b]
-    summed[1] = total
-    rings[lon] = total
-    for copy in sums2:
-        copy.start()
-    final = 1 - p
+    inside(p)
+    send_sum(1, get_sum(0))
 
     def emit(afters, x):
         for c, after in enumerate(afters):
             adjoint[c, x] = after
-            buf0[final, c, x + 1, own_rows, :] = after
-
-    accs = sweep(p, finish(), STEPS[1], emit=emit)
-
-    finish = exchange(accs)
+            wide0[c, x + 1, own_rows, :] = after
+
+    accs = rim_terms(p, finish(), STEPS[1], emit=emit)
+
+    finish = exchange(accs, wide0)
+    send_sum(2, get_sum(1))
     for _, wait in fwd_copies:
         wait()
     halo = finish()
@@ -1051,11 +1113,11 @@
         us = []
         rims, fwd_rims = rims_of(halo, 12, x), rims_of(fwd_halo, 12, x)
         for c in range(3):
-            u = buf0[final, c, x + 1, own_rows, :]
+            u = wide0[c, x + 1, own_rows, :]
             low_z, high_z = shifted(u, rims[4 * c : 4 * c + 4])
             ga.append([
-                buf0[final, c, x + 2, own_rows, :] * keep_x - u,
-                buf0[final, c, x + 1, pl.ds(TOP + 1, 32), :] * keep_y - u,
+                wide0[c, x + 2, own_rows, :] * keep_x - u,
+                wide0[c, x + 1, pl.ds(TOP + 1, 32), :] * keep_y - u,
                 high_z - u,
             ])
             us.append((u, low_z))
@@ -1067,8 +1129,8 @@
                 high_w - w,
             ])
         divergence = (
-            us[0][0] - edge(x, 0, 8) * buf0[final, 0, x, own_rows, :]
-            + (us[1][0] - edge_rows(0, 32) * buf0[final, 1, x + 1, pl.ds(TOP - 1, 32), :])
+            us[0][0] - edge(x, 0, 8) * wide0[0, x, own_rows, :]
+            + (us[1][0] - edge_rows(0, 32) * wide0[1, x + 1, pl.ds(TOP - 1, 32), :])
             + (us[2][0] - us[2][1])
         )
         pnext[x] = base[1, x + 1, own_rows, :] - v * divergence
@@ -1079,12 +1141,7 @@
         return carry
 
     lax.fori_loop(0, 8, outputs, 0, unroll=2)
-    for copy in sums2:
-        copy.wait()
-    total = rings[0]
-    for k in range(1, 8):
-        total = total + rings[k]
-    mean = jnp.sum(total) / CELLS
+    mean = jnp.sum(get_sum(2)) / CELLS
 
     def shift(x, carry):
         pnext[x] = pnext[x] - mean
@@ -1111,14 +1168,15 @@
             f32(2, 3, 10, 48, 128), f32(2, 4, 8, 128), f32(6, 256, 128), f32(6, 64, 128), f32(6, 16, 128),
             f32(6, 256, 128), f32(256, 128), f32(256, 128), f32(3, 256, 128), f32(3, 256, 128), f32(3, 8, 32, 128),
             f32(3, 10, 48, 128), f32(4, 8, 128), f32(3, 256, 128), f32(3, 10, 48, 128), f32(4, 8, 128),
+            f32(3, 10, 48, 128), f32(256, 128), f32(2, 2, 3, 32, 128), f32(2, 2, 3, 8, 8, 128),
             f32(4, 13, 48, 128), f32(4, 12, 40, 128), f32(12, 48, 128), f32(12, 40, 128),
             f32(3, 12, 48, 128), f32(3, 12, 48, 128), f32(3, 12, 40, 128),
             f32(2, 3, 12, 48, 128), f32(2, 3, 12, 40, 128), f32(3, 12, 48, 128), f32(3, 12, 40, 128),
-            f32(2, 2, 8, 128), f32(2, 3, 3, 2, 8, 128), f32(4, 6, 8, 128), f32(2, 4, 3, 3, 3, 8, 128),
+            f32(1, 2, 8, 128), f32(1, 3, 3, 2, 8, 128), f32(2, 4, 6, 8, 128), f32(2, 4, 3, 3, 3, 8, 128),
             f32(6, 48, 128), f32(6, 144, 128), f32(3, 8, 128), f32(1, 2, 8, 128),
-            f32(1, 8, 8, 128), f32(1, 64, 128), f32(2, 8, 128), f32(4, 8, 8, 128), f32(8, 8, 128),
-            dma(4), dma(2, 6), dma(2, 6), dma(3), dma(3), dma(1, 7), dma(1, 7), dma(1, 7), dma(1, 7), dma(31), dma(31), dma(7), dma(7),
-            dma(2, 26), dma(2, 26), dma(35), dma(35), dma(6), dma(6), dma(6), dma(6), dma(6), dma(6), dma(7), dma(7),
+            f32(1, 8, 8, 128), f32(1, 64, 128), f32(3, 8, 128), f32(4, 8, 128), f32(8, 8, 128), f32(8, 8, 128),
+            dma(4), dma(2, 6), dma(2, 6), dma(3), dma(3), dma(1, 7), dma(1, 7), dma(1, 7), dma(1, 7), dma(3, 7), dma(3, 7),
+            dma(1, 26), dma(1, 26), dma(35), dma(35), dma(6), dma(6), dma(6), dma(6), dma(2, 6), dma(2, 6), dma(7), dma(7),
         ],
         compiler_params=pltpu.CompilerParams(
             collective_id=0, has_side_effects=True, vmem_limit_bytes=60 * 1024 * 1024

time: 84.2 us -> 81.2 us (0.964)
  Pallas kernels: 80 us -> 76.6 us
    pallas_call x1, Pallas kernels: 80 us -> 76.6 us  [per_device(): pl.pallas_call(kernel, out_shape=(jax.ShapeDtypeStruct((3, 8, 32, 128), F...]
where the time goes in v4:
time: 81.2 us; the launch traced here: 80.6 us
  Pallas kernels  76.6 us (94%)
  local copies, waits for them, and re-layouts  3.41 us (4%)
    pallas_call x1, Pallas kernels, per_device(): pl.pallas_call(kernel, out_shape=(jax.ShapeDtypeStruct((3, 8, 32, 128), F...  76.6 us
    unnamed x7, local copies, waits for them, and re-layouts  3.41 us

profile of v4, /device:TPU:1, one launch (start us, length us, event | category | flops | bytes accessed | tf_op | source)
XLA Modules:
  0.0 80.6 jit_solution(11815423305727096915)
XLA Ops:
  0.6 76.6 %shard_map.76 = (f32[3,8,32,128]{3,2,1,0:T(8,128)}, f32[8,32,128]{2,1,0:T(8,128)}, f32[8,32,128]{2,1,0:T(8,128)}) custom-call(f32[3,8,32,128]{3,2,1,0:T(8,128)} %forcing.1, f32[8,32,128]{2,1,0:T(8,128)} %pressure.1, f32[8,32,128]{2,1,0:T(8,128)} %viscosity.1, f32[3,8,32,128]{3,2,1,0:T(8,128)} %forward.1, s32[2,8,32]{2,1,0:T(8,128)} %owner.1), custom_call_target="tpu_custom_call" | custom-call | tf_op jit(solution)/shard_map/pallas_call | solution.py:1157
  77.2 0.0 copy-start.1
  77.2 1.8 %copy.11 = f32[3,8,32,128]{3,2,1,0:T(8,128)} copy(f32[3,8,32,128]{3,2,1,0:T(8,128)} %get-tuple-element.6) | data formatting | bytes 786432
  79.0 0.0 copy-done.1
  79.0 0.0 copy-start
  79.0 0.7 copy.12
  79.7 0.3 copy-done
  80.0 0.7 copy.13
Async XLA Ops:
  77.2 1.8 %copy-start.1 = (f32[8,32,128]{2,1,0:T(8,128)S(1)}, f32[8,32,128]{2,1,0:T(8,128)}, u32[]{:S(2)}) copy-start(f32[8,32,128]{2,1,0:T(8,128)} %get-tuple-element.7) | copy-start | bytes 393220
  79.0 1.0 %copy-start = (f32[8,32,128]{2,1,0:T(8,128)S(1)}, f32[8,32,128]{2,1,0:T(8,128)}, u32[]{:S(2)}) copy-start(f32[8,32,128]{2,1,0:T(8,128)} %get-tuple-element.8) | copy-start | bytes 393220

commit v5 on v4

--- a/solution.py
+++ b/solution.py
@@ -51,8 +51,8 @@
     adjoint, pnext, gradient,
     load, base, fwd, base_z, fwd_z,
     buf0, zbuf, faces0, faces1, faces2, links0, diag0, inv0, res0, sol0, rim0, hbuf, hz, applied, mbuf, mz,
-    wide0, rim_link, halo_x, halo_y,
-    coef1, coef2, inv1, inv2, right1, left1, right2, deep1, deep2, sol1, sol2,
+    wide0, rim_link, halo_x, halo_y, strain,
+    coef1, coef2, inv1, inv2, right1, mid1, left1, right2, deep1, deep2, sol1, sol2,
     zsend1, zgot1, cz, dgot2,
     tmp, flat, erows, tile, got1, got2, summed, sum_x, sum_y, sum_z,
     in_sem, send_sem, recv_sem, fsend, frecv, send1, recv1, send2, recv2, sum_send, sum_recv,
@@ -180,14 +180,23 @@
         def start():
             pl.when(sends_it)(copy.start)
 
-        def wait():
+        def arrived():
+            pl.when(gets_it)(copy.wait_recv)
+
+        def left():
             pl.when(sends_it)(copy.wait_send)
-            pl.when(gets_it)(copy.wait_recv)
-
-        return start, wait
+
+        return start, arrived, left
 
     def plain(copy):
-        return copy.start, copy.wait
+        return copy.start, copy.wait_recv, copy.wait_send
+
+    unsettled = []
+
+    def settle():
+        for left in unsettled:
+            left()
+        unsettled.clear()
 
     def sends(buf, zref, ssem, rsem, beside=None):
         rows, planes = pl.ds(TOP, 32), pl.ds(1, 8)
@@ -215,12 +224,14 @@
     def send_all(accs, buf, zref, ssem, rsem, beside=None):
         zref[0], zref[1] = accs
         copies = sends(buf, zref, ssem, rsem, beside)
-        for start, _ in copies:
+        for start, _, _ in copies:
             start()
+        settle()
 
         def finish():
-            for _, wait in copies:
-                wait()
+            for _, arrived, left in copies:
+                arrived()
+                unsettled.append(left)
             return merged(zref[2], zref[3])
 
         return finish
@@ -256,7 +267,7 @@
         for i, (src, dst, target) in enumerate(fwd_parts)
     ]
     fwd_copies = [guarded(fwd_copies[0], -1)] + [plain(copy) for copy in fwd_copies[1:]]
-    for begin, _ in fwd_copies:
+    for begin, _, _ in fwd_copies:
         begin()
 
     grid_row, grid_lane = rows_of((128, 128)), lanes_of((128, 128))
@@ -411,10 +422,13 @@
         each(0, lambda copy: copy.start())
 
         def finish(low_plane, high_plane):
-            for way, sends_it, gets_it in ((1, rad < 3, rad > 0), (-1, rad > 0, rad < 3)):
+            for way, gets_it in ((1, rad > 0), (-1, rad < 3)):
+                pl.when(gets_it)(lambda way=way: each(way, lambda copy: copy.wait_recv()))
+            each(0, lambda copy: copy.wait_recv())
+
+            for way, sends_it in ((1, rad < 3), (-1, rad > 0)):
                 pl.when(sends_it)(lambda way=way: each(way, lambda copy: copy.wait_send()))
-                pl.when(gets_it)(lambda way=way: each(way, lambda copy: copy.wait_recv()))
-            each(0, lambda copy: copy.wait())
+            each(0, lambda copy: copy.wait_send())
 
             def one(plane, carry):
                 dx, x = lax.div(plane, 4), lax.rem(plane, 4)
@@ -442,12 +456,13 @@
         n = ref.shape[0]
 
         def go(copies):
-            for start, _ in copies:
+            for start, _, _ in copies:
                 start()
 
         def done(copies):
-            for _, wait in copies:
-                wait()
+            for _, arrived, left in copies:
+                arrived()
+                left()
 
         def copy(i, src, dst, target):
             return remote(src, dst, csend1.at[use, i], crecv1.at[use, i], target)
@@ -558,7 +573,8 @@
 
         def finish():
             for copy in copies:
-                copy.wait()
+                copy.wait_recv()
+                unsettled.append(copy.wait_send)
 
         return finish
 
@@ -638,7 +654,7 @@
                 deep[1 - p, c, x, here, :] = update
             return carry
 
-        lax.fori_loop(planes[0], planes[1], one, 0, unroll=2)
+        lax.fori_loop(planes[0], planes[1], one, 0, unroll=4 if (planes[1] - planes[0]) % 4 == 0 else 2)
 
     def inside(p, first=False):
         def plane(x, carry):
@@ -656,7 +672,7 @@
                 sol0[c, at, :] = v if first else sol0[c, at, :] + v
             return carry
 
-        lax.fori_loop(0, 8, plane, 0, unroll=2)
+        lax.fori_loop(0, 8, plane, 0, unroll=4)
 
     def rim_terms(p, halo, step, emit=None):
         for side, rows in ((0, pl.ds(0, 32)), (1, pl.ds(224, 32))):
@@ -691,7 +707,7 @@
                 emit(packs, x)
             return pack(accs, packs, x)
 
-        return lax.fori_loop(0, 8, plane, (zero8, zero8), unroll=2)
+        return lax.fori_loop(0, 8, plane, (zero8, zero8), unroll=4)
 
     def correct(p):
         def plane(x, accs):
@@ -749,7 +765,8 @@
 
         def middle():
             for copy in first:
-                copy.wait()
+                copy.wait_recv()
+                unsettled.append(copy.wait_send)
             total = got1[use, 0]
             for k in range(1, 8):
                 total = total + got1[use, k]
@@ -760,7 +777,8 @@
 
         def end():
             for copy in second:
-                copy.wait()
+                copy.wait_recv()
+                unsettled.append(copy.wait_send)
 
         return begin, middle, end
 
@@ -973,14 +991,15 @@
     weigh_all()
     finish(1, 11)
     begin_deep(1, right1, (1, 11), None)
-    sweep_deep(1, 0, right1, right1, (2, 10), STEPS[0])
-    sweep_deep(1, 1, right1, right1, (3, 9), STEPS[1])
-    sweep_deep(1, 0, right1, left1, (4, 8), None, rows=(16, 16))
+    sweep_deep(1, 0, right1, mid1, (2, 10), STEPS[0])
+    sweep_deep(1, 1, mid1, mid1, (3, 9), STEPS[1])
+    sweep_deep(1, 0, mid1, left1, (4, 8), None, rows=(16, 16))
 
     sums = restrict(lambda c, x: left1[c, 4 + x, OWN1, :], 16, 1, own_pair)
     finish2 = exchange2(1, packed2([sums[16 * c + 8 * x : 16 * c + 8 * x + 8] for c in range(3) for x in range(2)]))
     rest = layers1(1, left1, 3, 3)
     rest[0]()
+    settle()
     pending["coef2"](3)
     unpack2(0, coef2)
     invert(coef2, inv2, 12)
@@ -994,9 +1013,39 @@
     sweep_deep(2, 1, right2, right2, all2, STEPS[1])
     sweep_deep(2, 0, right2, right2, all2, None)
 
+    def forward_strain():
+        for _, arrived, left in fwd_copies:
+            arrived()
+            left()
+        fwd_halo = merged(zero8, fwd_z[1])
+
+        def one(x, carry):
+            at = block(x, 32)
+            v = base[0, x + 1, own_rows, :]
+            keep_x, keep_y = edge(x, 1, 8), edge_rows(1, 32)
+            rims = rims_of(fwd_halo, 12, x)
+            gf = []
+            for c in range(3):
+                w = fwd[c, x + 1, own_rows, :]
+                _, high_w = shifted(w, rims[4 * c : 4 * c + 4])
+                gf.append([
+                    fwd[c, x + 2, own_rows, :] * keep_x - w,
+                    fwd[c, x + 1, pl.ds(TOP + 1, 32), :] * keep_y - w,
+                    high_w - w,
+                ])
+            for c in range(3):
+                strain[c, at, :] = 2.0 * v * gf[c][c]
+            for i, (d, e) in enumerate(((0, 1), (0, 2), (1, 2))):
+                strain[3 + i, at, :] = v * (gf[e][d] + gf[d][e])
+            return carry
+
+        lax.fori_loop(0, 8, one, 0)
+
     def while_along():
         rest[2]()
+        settle()
         apply_to_m()
+        forward_strain()
 
     coarse_solve((while_along, rest[3]))
     sweep_deep(2, 1, right2, right2, all2, STEPS[0], initial=True)
@@ -1061,7 +1110,7 @@
 
     partial = lax.fori_loop(0, 8, add_up, zero8, unroll=2)
     rounds = []
-    for i, (got, at, targets) in enumerate(((sum_x, rad, through), (sum_y, lat, across), (sum_z, lon, along))):
+    for i, (got, at, targets) in enumerate(((sum_z, lon, along), (sum_y, lat, across), (sum_x, rad, through))):
         copies = [
             remote(summed.at[i], got.at[at], sum_send.at[i, k], sum_recv.at[i, k], target)
             for k, target in enumerate(targets)
@@ -1078,7 +1127,8 @@
     def get_sum(i):
         got, _, copies = rounds[i]
         for copy in copies:
-            copy.wait()
+            copy.wait_recv()
+            unsettled.append(copy.wait_send)
         total = got[0]
         for k in range(1, len(copies) + 1):
             total = total + got[k]
@@ -1101,17 +1151,13 @@
 
     finish = exchange(accs, wide0)
     send_sum(2, get_sum(1))
-    for _, wait in fwd_copies:
-        wait()
     halo = finish()
-    fwd_halo = merged(zero8, fwd_z[1])
 
     def outputs(x, carry):
         v = base[0, x + 1, own_rows, :]
         keep_x, keep_y = edge(x, 1, 8), edge_rows(1, 32)
-        ga, gf = [], []
-        us = []
-        rims, fwd_rims = rims_of(halo, 12, x), rims_of(fwd_halo, 12, x)
+        ga, us = [], []
+        rims = rims_of(halo, 12, x)
         for c in range(3):
             u = wide0[c, x + 1, own_rows, :]
             low_z, high_z = shifted(u, rims[4 * c : 4 * c + 4])
@@ -1121,27 +1167,22 @@
                 high_z - u,
             ])
             us.append((u, low_z))
-            w = fwd[c, x + 1, own_rows, :]
-            _, high_w = shifted(w, fwd_rims[4 * c : 4 * c + 4])
-            gf.append([
-                fwd[c, x + 2, own_rows, :] * keep_x - w,
-                fwd[c, x + 1, pl.ds(TOP + 1, 32), :] * keep_y - w,
-                high_w - w,
-            ])
         divergence = (
             us[0][0] - edge(x, 0, 8) * wide0[0, x, own_rows, :]
             + (us[1][0] - edge_rows(0, 32) * wide0[1, x + 1, pl.ds(TOP - 1, 32), :])
             + (us[2][0] - us[2][1])
         )
         pnext[x] = base[1, x + 1, own_rows, :] - v * divergence
-        summed = gf[0][0] * ga[0][0] + gf[1][1] * ga[1][1] + gf[2][2] * ga[2][2]
-        for d, e in ((0, 1), (0, 2), (1, 2)):
-            summed = summed + 0.5 * (gf[e][d] + gf[d][e]) * (ga[e][d] + ga[d][e])
-        gradient[x] = 2.0 * v * summed
+        at = block(x, 32)
+        total = strain[0, at, :] * ga[0][0] + strain[1, at, :] * ga[1][1] + strain[2, at, :] * ga[2][2]
+        for i, (d, e) in enumerate(((0, 1), (0, 2), (1, 2))):
+            total = total + strain[3 + i, at, :] * (ga[e][d] + ga[d][e])
+        gradient[x] = total
         return carry
 
     lax.fori_loop(0, 8, outputs, 0, unroll=2)
     mean = jnp.sum(get_sum(2)) / CELLS
+    settle()
 
     def shift(x, carry):
         pnext[x] = pnext[x] - mean
@@ -1168,9 +1209,9 @@
             f32(2, 3, 10, 48, 128), f32(2, 4, 8, 128), f32(6, 256, 128), f32(6, 64, 128), f32(6, 16, 128),
             f32(6, 256, 128), f32(256, 128), f32(256, 128), f32(3, 256, 128), f32(3, 256, 128), f32(3, 8, 32, 128),
             f32(3, 10, 48, 128), f32(4, 8, 128), f32(3, 256, 128), f32(3, 10, 48, 128), f32(4, 8, 128),
-            f32(3, 10, 48, 128), f32(256, 128), f32(2, 2, 3, 32, 128), f32(2, 2, 3, 8, 8, 128),
+            f32(3, 10, 48, 128), f32(256, 128), f32(2, 2, 3, 32, 128), f32(2, 2, 3, 8, 8, 128), f32(6, 256, 128),
             f32(4, 13, 48, 128), f32(4, 12, 40, 128), f32(12, 48, 128), f32(12, 40, 128),
-            f32(3, 12, 48, 128), f32(3, 12, 48, 128), f32(3, 12, 40, 128),
+            f32(3, 12, 48, 128), f32(3, 12, 48, 128), f32(3, 12, 48, 128), f32(3, 12, 40, 128),
             f32(2, 3, 12, 48, 128), f32(2, 3, 12, 40, 128), f32(3, 12, 48, 128), f32(3, 12, 40, 128),
             f32(1, 2, 8, 128), f32(1, 3, 3, 2, 8, 128), f32(2, 4, 6, 8, 128), f32(2, 4, 3, 3, 3, 8, 128),
             f32(6, 48, 128), f32(6, 144, 128), f32(3, 8, 128), f32(1, 2, 8, 128),

time: 81.2 us -> 77 us (0.948)
  Pallas kernels: 76.6 us -> 72.7 us
    pallas_call x1, Pallas kernels: 76.6 us -> 72.7 us  [per_device(): pl.pallas_call(kernel, out_shape=(jax.ShapeDtypeStruct((3, 8, 32, 128), F...]
where the time goes in v5:
time: 77 us; the launch traced here: 76.8 us
  Pallas kernels  72.7 us (94%)
  local copies, waits for them, and re-layouts  3.41 us (4%)
    pallas_call x1, Pallas kernels, per_device(): pl.pallas_call(kernel, out_shape=(jax.ShapeDtypeStruct((3, 8, 32, 128), F...  72.7 us
    unnamed x7, local copies, waits for them, and re-layouts  3.41 us

profile of v5, /device:TPU:1, one launch (start us, length us, event | category | flops | bytes accessed | tf_op | source)
XLA Modules:
  0.0 76.8 jit_solution(16421872232264855285)
XLA Ops:
  0.6 72.7 %shard_map.76 = (f32[3,8,32,128]{3,2,1,0:T(8,128)}, f32[8,32,128]{2,1,0:T(8,128)}, f32[8,32,128]{2,1,0:T(8,128)}) custom-call(f32[3,8,32,128]{3,2,1,0:T(8,128)} %forcing.1, f32[8,32,128]{2,1,0:T(8,128)} %pressure.1, f32[8,32,128]{2,1,0:T(8,128)} %viscosity.1, f32[3,8,32,128]{3,2,1,0:T(8,128)} %forward.1, s32[2,8,32]{2,1,0:T(8,128)} %owner.1), custom_call_target="tpu_custom_call" | custom-call | tf_op jit(solution)/shard_map/pallas_call | solution.py:1198
  73.4 0.0 copy-start.1
  73.4 1.8 %copy.11 = f32[3,8,32,128]{3,2,1,0:T(8,128)} copy(f32[3,8,32,128]{3,2,1,0:T(8,128)} %get-tuple-element.6) | data formatting | bytes 786432
  75.2 0.0 copy-done.1
  75.2 0.0 copy-start
  75.2 0.7 copy.12
  75.8 0.3 copy-done
  76.1 0.7 copy.13
Async XLA Ops:
  73.4 1.8 %copy-start.1 = (f32[8,32,128]{2,1,0:T(8,128)S(1)}, f32[8,32,128]{2,1,0:T(8,128)}, u32[]{:S(2)}) copy-start(f32[8,32,128]{2,1,0:T(8,128)} %get-tuple-element.7) | copy-start | bytes 393220
  75.2 1.0 %copy-start = (f32[8,32,128]{2,1,0:T(8,128)S(1)}, f32[8,32,128]{2,1,0:T(8,128)}, u32[]{:S(2)}) copy-start(f32[8,32,128]{2,1,0:T(8,128)} %get-tuple-element.8) | copy-start | bytes 393220

commit v6 on v5

--- a/solution.py
+++ b/solution.py
@@ -730,7 +730,7 @@
                 packs.append(update)
             return pack(accs, packs, x)
 
-        return lax.fori_loop(0, 8, plane, (zero8, zero8), unroll=2)
+        return lax.fori_loop(0, 8, plane, (zero8, zero8), unroll=4)
 
     def restrict(source, rows, level, matrix):
         nx, ny, _ = LEVELS[level]
@@ -1180,7 +1180,7 @@
         gradient[x] = total
         return carry
 
-    lax.fori_loop(0, 8, outputs, 0, unroll=2)
+    lax.fori_loop(0, 8, outputs, 0, unroll=4)
     mean = jnp.sum(get_sum(2)) / CELLS
     settle()
 

time: 77 us -> 76.5 us (level)
  no operation moved by 1% of the time
where the time goes in v6:
time: 76.5 us; the launch traced here: 76.2 us
  Pallas kernels  72.2 us (94%)
  local copies, waits for them, and re-layouts  3.41 us (4%)
    pallas_call x1, Pallas kernels, per_device(): pl.pallas_call(kernel, out_shape=(jax.ShapeDtypeStruct((3, 8, 32, 128), F...  72.2 us
    unnamed x7, local copies, waits for them, and re-layouts  3.41 us

profile of v6, /device:TPU:1, one launch (start us, length us, event | category | flops | bytes accessed | tf_op | source)
XLA Modules:
  0.0 76.2 jit_solution(5169587483923325568)
XLA Ops:
  0.6 72.2 %shard_map.76 = (f32[3,8,32,128]{3,2,1,0:T(8,128)}, f32[8,32,128]{2,1,0:T(8,128)}, f32[8,32,128]{2,1,0:T(8,128)}) custom-call(f32[3,8,32,128]{3,2,1,0:T(8,128)} %forcing.1, f32[8,32,128]{2,1,0:T(8,128)} %pressure.1, f32[8,32,128]{2,1,0:T(8,128)} %viscosity.1, f32[3,8,32,128]{3,2,1,0:T(8,128)} %forward.1, s32[2,8,32]{2,1,0:T(8,128)} %owner.1), custom_call_target="tpu_custom_call" | custom-call | tf_op jit(solution)/shard_map/pallas_call | solution.py:1198
  72.8 0.0 copy-start.1
  72.8 1.8 %copy.11 = f32[3,8,32,128]{3,2,1,0:T(8,128)} copy(f32[3,8,32,128]{3,2,1,0:T(8,128)} %get-tuple-element.6) | data formatting | bytes 786432
  74.6 0.0 copy-done.1
  74.6 0.0 copy-start
  74.6 0.7 copy.12
  75.3 0.3 copy-done
  75.6 0.7 copy.13
Async XLA Ops:
  72.8 1.8 %copy-start.1 = (f32[8,32,128]{2,1,0:T(8,128)S(1)}, f32[8,32,128]{2,1,0:T(8,128)}, u32[]{:S(2)}) copy-start(f32[8,32,128]{2,1,0:T(8,128)} %get-tuple-element.7) | copy-start | bytes 393220
  74.6 1.0 %copy-start = (f32[8,32,128]{2,1,0:T(8,128)S(1)}, f32[8,32,128]{2,1,0:T(8,128)}, u32[]{:S(2)}) copy-start(f32[8,32,128]{2,1,0:T(8,128)} %get-tuple-element.8) | copy-start | bytes 393220
